TPU v7x, 32 devices: a whole 2x2x4 slice. The times are simulated.
32 devices in a mesh: groups: 2 (over x), expert: 16 (over z, y, core).
Axes of the slice: x: 2, y: 2, z: 4, core: 2. Of those that a mesh axis runs over, the one named last changes fastest.
Arguments:
- tokens: bfloat16 [2048, 2048], P(('groups', 'expert')), parts along dimension 0, may hold values from -6 to 6
- out_grad: bfloat16 [2048, 2048], P(('groups', 'expert')), parts along dimension 0, may hold values from -6 to 6
- routes: int32 [2048, 8], P(('groups', 'expert')), parts along dimension 0, may hold values from 0 to 15, all different within a row; in each aligned block of 64 rows (0 to 63, 64 to 127, ...) at most 40 rows name the same one
- route_weights: bfloat16 [2048, 8], P(('groups', 'expert')), parts along dimension 0, may hold values from 0.049804688 to 0.29882812
- gate_weight: bfloat16 [16, 2048, 768], P('expert'), may hold values from -0.125 to 0.125
- up_weight: bfloat16 [16, 2048, 768], P('expert'), may hold values from -0.125 to 0.125
- down_weight: bfloat16 [16, 768, 2048], P('expert'), may hold values from -0.21875 to 0.21875
- gate_adapter_input: bfloat16 [16, 16, 2048], P('expert'), may hold values from -0.125 to 0.125
- gate_adapter_output: bfloat16 [16, 16, 768], P('expert'), may hold values from -1.5 to 1.5
- up_adapter_input: bfloat16 [16, 16, 2048], P('expert'), may hold values from -0.125 to 0.125
- up_adapter_output: bfloat16 [16, 16, 768], P('expert'), may hold values from -1.5 to 1.5
- down_adapter_input: bfloat16 [16, 16, 768], P('expert'), may hold values from -0.21875 to 0.21875
- down_adapter_output: bfloat16 [16, 16, 2048], P('expert'), may hold values from -1.5 to 1.5
Outputs:
- grad_tokens: bfloat16 [2048, 2048], P(('groups', 'expert')), parts along dimension 0
- grad_weights: float32 [2048, 8], P(('groups', 'expert')), parts along dimension 0
- grad_a_gate: float32 [32, 16, 2048], P(('groups', 'expert')), parts along dimension 0
- grad_b_gate: float32 [32, 16, 768], P(('groups', 'expert')), parts along dimension 0
- grad_a_up: float32 [32, 16, 2048], P(('groups', 'expert')), parts along dimension 0
- grad_b_up: float32 [32, 16, 768], P(('groups', 'expert')), parts along dimension 0
- grad_a_down: float32 [32, 16, 768], P(('groups', 'expert')), parts along dimension 0
- grad_b_down: float32 [32, 16, 2048], P(('groups', 'expert')), parts along dimension 0
There are 2 independent parts, one for each index of `groups`. A program takes and returns all parts, laid end to end along the dimension named above; an argument that names none is the same for every part. Nothing has to cross between parts.
Inputs may be any that keep to these rules, and one draw needn't show every extreme that they name: `routes`: each row names 8 different experts, and every expert is named by some row. Among the rows of one index of expert (aligned blocks of 64 rows), no expert is named more than 40 times, a bound that some block reaches.
All inputs are finite; a program needn't handle non-finite values.
Results may differ from a plain program's by a relative error of at most 0.0068.
Values may be sent and summed in bfloat16 or wider, within the bound.
A program may use at most 128 MiB of HBM per device.

v0:
```python
import jax
import jax.numpy as jnp
from jax import lax
from jax.sharding import PartitionSpec as P

ADAPTER_SCALING = 0.5


def slot_ranks(id_block, expert_count):
    flat_ids = id_block.reshape(-1)
    one_hot = (flat_ids[:, None] == jnp.arange(expert_count, dtype=jnp.int32)[None, :]).astype(
        jnp.int32
    )
    earlier = jnp.cumsum(one_hot, 0) - one_hot
    return jnp.sum(earlier * one_hot, 1).reshape(id_block.shape)


def low_rank(factor_matrix, multiplier):
    return lax.dot_general(
        factor_matrix, multiplier, (((1,), (1,)), ((), ())), preferred_element_type=jnp.float32
    ).astype(jnp.bfloat16)


def outer_sum(factor_matrix, multiplier):
    return ADAPTER_SCALING * lax.dot_general(
        factor_matrix, multiplier, (((0,), (0,)), ((), ())), preferred_element_type=jnp.float32
    )


def expert_backward(
    input_rows,
    rows_grad,
    rows_weight,
    gate_weight,
    up_weight,
    down_weight,
    gate_adapter_input,
    gate_adapter_output,
    up_adapter_input,
    up_adapter_output,
    down_adapter_input,
    down_adapter_output,
):
    gate_reduced = low_rank(input_rows, gate_adapter_input)
    up_reduced = low_rank(input_rows, up_adapter_input)
    gate_preactivation = jnp.dot(
        input_rows, gate_weight, preferred_element_type=jnp.float32
    ) + ADAPTER_SCALING * jnp.dot(
        gate_reduced, gate_adapter_output, preferred_element_type=jnp.float32
    )
    up_preactivation = jnp.dot(
        input_rows, up_weight, preferred_element_type=jnp.float32
    ) + ADAPTER_SCALING * jnp.dot(up_reduced, up_adapter_output, preferred_element_type=jnp.float32)
    sigmoid_gate = jax.nn.sigmoid(gate_preactivation)
    activated = gate_preactivation * sigmoid_gate
    hidden_state = (activated * up_preactivation).astype(jnp.bfloat16)
    hidden_reduced = low_rank(hidden_state, down_adapter_input)
    expert_result = (
        jnp.dot(hidden_state, down_weight, preferred_element_type=jnp.float32)
        + ADAPTER_SCALING
        * jnp.dot(hidden_reduced, down_adapter_output, preferred_element_type=jnp.float32)
    ).astype(jnp.bfloat16)
    position_gradient = (
        rows_weight.astype(jnp.float32)[:, None] * rows_grad.astype(jnp.float32)
    ).astype(jnp.bfloat16)
    reduced_gradient = low_rank(position_gradient, down_adapter_output)
    hidden_gradient = lax.dot_general(
        position_gradient, down_weight, (((1,), (1,)), ((), ())), preferred_element_type=jnp.float32
    ) + ADAPTER_SCALING * jnp.dot(
        reduced_gradient, down_adapter_input, preferred_element_type=jnp.float32
    )
    grad_gate = (
        hidden_gradient
        * up_preactivation
        * sigmoid_gate
        * (1.0 + gate_preactivation * (1.0 - sigmoid_gate))
    ).astype(jnp.bfloat16)
    grad_up = (hidden_gradient * activated).astype(jnp.bfloat16)
    gate_reduced_gradient = low_rank(grad_gate, gate_adapter_output)
    up_reduced_gradient = low_rank(grad_up, up_adapter_output)
    gradient_rows = lax.dot_general(
        grad_gate, gate_weight, (((1,), (1,)), ((), ())), preferred_element_type=jnp.float32
    )
    gradient_rows = gradient_rows + lax.dot_general(
        grad_up, up_weight, (((1,), (1,)), ((), ())), preferred_element_type=jnp.float32
    )
    gradient_rows = gradient_rows + ADAPTER_SCALING * (
        jnp.dot(gate_reduced_gradient, gate_adapter_input, preferred_element_type=jnp.float32)
        + jnp.dot(up_reduced_gradient, up_adapter_input, preferred_element_type=jnp.float32)
    )
    adapter_grads = (
        outer_sum(gate_reduced_gradient, input_rows),
        outer_sum(gate_reduced, grad_gate),
        outer_sum(up_reduced_gradient, input_rows),
        outer_sum(up_reduced, grad_up),
        outer_sum(reduced_gradient, hidden_state),
        outer_sum(hidden_reduced, position_gradient),
    )
    return (gradient_rows.astype(jnp.bfloat16), expert_result, adapter_grads)


def shards(
    tokens,
    out_grad,
    routes,
    route_weights,
    gate_weight,
    up_weight,
    down_weight,
    gate_adapter_input,
    gate_adapter_output,
    up_adapter_input,
    up_adapter_output,
    down_adapter_input,
    down_adapter_output,
):
    tok_rows, features = tokens.shape
    top_count = routes.shape[1]
    peer_count = lax.axis_size("expert")
    experts = peer_count * gate_weight.shape[0]
    capacity = tok_rows * top_count * 5 // (4 * experts)
    targets = routes * capacity + slot_ranks(routes, experts)
    matches = jnp.arange(experts * capacity, dtype=jnp.int32)[:, None, None] == targets[None, :, :]
    placing = jnp.any(matches, -1).astype(jnp.bfloat16)
    slot_weight = jnp.sum(
        jnp.where(matches, route_weights.astype(jnp.float32)[None, :, :], 0.0), (1, 2)
    ).astype(jnp.bfloat16)
    sent_rows = jnp.dot(placing, tokens, preferred_element_type=jnp.float32).astype(jnp.bfloat16)
    sent_grads = jnp.dot(placing, out_grad, preferred_element_type=jnp.float32).astype(jnp.bfloat16)
    got_rows, got_grads, got_weight = (
        lax.all_to_all(
            sent_rows.reshape(experts, capacity, features),
            "expert",
            split_axis=0,
            concat_axis=0,
            tiled=True,
        ),
        lax.all_to_all(
            sent_grads.reshape(experts, capacity, features),
            "expert",
            split_axis=0,
            concat_axis=0,
            tiled=True,
        ),
        lax.all_to_all(
            slot_weight.reshape(experts, capacity),
            "expert",
            split_axis=0,
            concat_axis=0,
            tiled=True,
        ),
    )
    gradient_rows, expert_result, adapter_grads = expert_backward(
        got_rows.reshape(-1, features),
        got_grads.reshape(-1, features),
        got_weight.reshape(-1),
        gate_weight[0],
        up_weight[0],
        down_weight[0],
        gate_adapter_input[0],
        gate_adapter_output[0],
        up_adapter_input[0],
        up_adapter_output[0],
        down_adapter_input[0],
        down_adapter_output[0],
    )
    dots_here = jnp.sum(
        got_grads.reshape(-1, features).astype(jnp.float32) * expert_result.astype(jnp.float32), -1
    )
    back_rows = lax.all_to_all(
        gradient_rows.reshape(peer_count, capacity, features),
        "expert",
        split_axis=0,
        concat_axis=0,
        tiled=True,
    )
    slot_dots = lax.all_to_all(
        dots_here.reshape(peer_count, capacity), "expert", split_axis=0, concat_axis=0, tiled=True
    ).reshape(-1)
    grad_tokens = lax.dot_general(
        placing,
        back_rows.reshape(-1, features),
        (((0,), (0,)), ((), ())),
        preferred_element_type=jnp.float32,
    ).astype(jnp.bfloat16)
    grad_weights = jnp.take(slot_dots, targets.reshape(-1)).reshape(tok_rows, top_count)
    return (
        grad_tokens,
        grad_weights,
        adapter_grads[0][None],
        adapter_grads[1][None],
        adapter_grads[2][None],
        adapter_grads[3][None],
        adapter_grads[4][None],
        adapter_grads[5][None],
    )


def solution(mesh):
    return jax.shard_map(
        shards,
        mesh=mesh,
        in_specs=(
            P(("groups", "expert"), None),
            P(("groups", "expert"), None),
            P(("groups", "expert"), None),
            P(("groups", "expert"), None),
            P("expert", None, None),
            P("expert", None, None),
            P("expert", None, None),
            P("expert", None, None),
            P("expert", None, None),
            P("expert", None, None),
            P("expert", None, None),
            P("expert", None, None),
            P("expert", None, None),
        ),
        out_specs=(
            P(("groups", "expert"), None),
            P(("groups", "expert"), None),
            P(("groups", "expert"), None, None),
            P(("groups", "expert"), None, None),
            P(("groups", "expert"), None, None),
            P(("groups", "expert"), None, None),
            P(("groups", "expert"), None, None),
            P(("groups", "expert"), None, None),
        ),
        check_vma=False,
    )
```

profile of v0, /device:TPU:15, one launch (start us, length us, event | category | flops | bytes accessed | tf_op | source)
XLA Modules:
  0.0 251.8 jit_solution(17982594361336717080)
XLA Ops:
  0.6 0.9 copy.53
  1.6 0.1 eq.43
  1.7 0.1 eq.39
  1.8 1.2 reduce-window.6
  2.9 0.2 slice_reduce_fusion
  3.2 0.1 fusion.32
  3.3 0.1 reshape.144
  3.4 0.1 copy.56
  3.4 0.7 multiply_add_fusion.3
  4.1 0.1 copy.57
  4.2 0.8 copy.58
  5.0 0.2 select_reduce_fusion
  5.2 0.7 convert_element_type.139
  5.9 6.6 %all-to-all-start = ((bf16[16,1,40]{2,1,0:T(2,128)(2,1)}), bf16[16,1,40]{2,1,0:T(2,128)(2,1)S(1)}, u32[]{:S(2)}, u32[]{:S(2)}) async-start(bf16[16,1,40]{2,1,0:T(2,128)(2,1)} %convert_element_type.139), calls=%async_computation | async-start | bytes 16384 | tf_op jit(solution)/shard_map/all_to_all | solution.py:145
  12.5 0.5 fusion.19
  12.9 3.4 %convolution_convert_fusion = bf16[640,2048]{1,0:T(8,128)(2,1)} fusion(pred[640,64]{0,1:T(8,128)(4,1)S(1)} %fusion.19, bf16[64,2048]{1,0:T(8,128)(2,1)} %param.13), kind=kOutput, calls=%fused_computation.9 | convolution fusion | flops 169082880 | bytes 2924544 | tf_op jit(solution)/shard_map/dot_general | solution.py:128
  16.3 7.0 %all-to-all-start.2 = ((bf16[16,40,2048]{2,1,0:T(8,128)(2,1)}), bf16[16,40,2048]{2,1,0:T(8,128)(2,1)}, u32[]{:S(2)}, u32[]{:S(2)}) async-start(bf16[16,40,2048]{2,1,0:T(8,128)(2,1)} %bitcast.130), calls=%async_computation.2 | async-start | bytes 5242880 | tf_op jit(solution)/shard_map/all_to_all | solution.py:131
  23.3 2.4 convolution_convert_fusion.1
  25.7 56.4 %all-to-all-done.2 = bf16[16,40,2048]{2,1,0:T(8,128)(2,1)} async-done(((bf16[16,40,2048]{2,1,0:T(8,128)(2,1)}), bf16[16,40,2048]{2,1,0:T(8,128)(2,1)}, u32[]{:S(2)}, u32[]{:S(2)}) %all-to-all-start.2) | async-done | bytes 2621472 | tf_op jit(solution)/shard_map/all_to_all | solution.py:131
  82.1 5.0 %all-to-all-start.1 = ((bf16[16,40,2048]{2,1,0:T(8,128)(2,1)}), bf16[16,40,2048]{2,1,0:T(8,128)(2,1)}, u32[]{:S(2)}, u32[]{:S(2)}) async-start(bf16[16,40,2048]{2,1,0:T(8,128)(2,1)} %bitcast.129), calls=%async_computation.1 | async-start | bytes 5242880 | tf_op jit(solution)/shard_map/all_to_all | solution.py:138
  87.1 2.7 %convolution_convert_fusion.6 = bf16[640,16]{0,1:T(8,128)(2,1)S(1)} fusion(bf16[640,2048]{1,0:T(8,128)(2,1)} %bitcast.8, bf16[1,16,2048]{2,1,0:T(8,128)(2,1)S(1)} %copy-done.7), kind=kOutput, calls=%fused_computation.50 | convolution fusion | flops 41953280 | bytes 2707456 | tf_op jit(solution)/shard_map/dot_general | solution.py:19
  89.8 2.5 %convolution_convert_fusion.7 = bf16[640,16]{0,1:T(8,128)(2,1)S(1)} fusion(bf16[640,2048]{1,0:T(8,128)(2,1)} %bitcast.8, bf16[1,16,2048]{2,1,0:T(8,128)(2,1)S(1)} %copy-done.8), kind=kOutput, calls=%fused_computation.51 | convolution fusion | flops 41953280 | bytes 2707456 | tf_op jit(solution)/shard_map/dot_general | solution.py:19
  92.3 5.2 %fusion.5 = f32[640,768]{1,0:T(8,128)} fusion(bf16[640,2048]{1,0:T(8,128)(2,1)} %bitcast.8, bf16[1,2048,768]{2,1,0:T(8,128)(2,1)S(1)} %copy-done.12), kind=kOutput, calls=%fused_computation.13 | convolution fusion | flops 2013265920 | bytes 7733248 | tf_op jit(solution)/shard_map/dot_general | solution.py:46
  97.6 5.2 %fusion.9 = f32[640,768]{1,0:T(8,128)} fusion(bf16[640,2048]{1,0:T(8,128)(2,1)} %bitcast.8, bf16[1,2048,768]{2,1,0:T(8,128)(2,1)S(1)} %copy-done), kind=kOutput, calls=%fused_computation.17 | convolution fusion | flops 2013265920 | bytes 7733248 | tf_op jit(solution)/shard_map/dot_general | solution.py:51
  102.8 43.0 %all-to-all-done.1 = bf16[16,40,2048]{2,1,0:T(8,128)(2,1)} async-done(((bf16[16,40,2048]{2,1,0:T(8,128)(2,1)}), bf16[16,40,2048]{2,1,0:T(8,128)(2,1)}, u32[]{:S(2)}, u32[]{:S(2)}) %all-to-all-start.1) | async-done | bytes 2621472 | tf_op jit(solution)/shard_map/all_to_all | solution.py:138
  145.8 2.4 fusion
  148.2 0.8 convolution_convert_fusion.8
  149.0 2.2 fusion.13
  151.3 0.5 multiply_add_fusion
  151.8 0.3 copy-done.10
  152.1 0.5 multiply_add_fusion.2
  152.5 0.3 copy-done.11
  152.8 0.8 copy-done.15
  153.6 1.3 multiply_convert_fusion
  154.9 0.4 convolution_convert_fusion.4
  155.3 4.6 %fusion.7 = f32[640,2048]{1,0:T(8,128)} fusion(bf16[640,768]{1,0:T(8,128)(2,1)S(1)} %get-tuple-element.42, bf16[1,2048,768]{2,1,0:T(8,128)(2,1)S(1)} %copy-done), kind=kOutput, calls=%fused_computation.15 | convolution fusion | flops 2013265920 | bytes 9371648 | tf_op jit(solution)/shard_map/dot_general | solution.py:84
  159.9 0.4 convolution_convert_fusion.5
  160.2 4.8 %fusion.3 = f32[640,2048]{1,0:T(8,128)} fusion(bf16[640,768]{1,0:T(8,128)(2,1)S(1)} %get-tuple-element.41, bf16[1,2048,768]{2,1,0:T(8,128)(2,1)S(1)} %copy-done.13), kind=kOutput, calls=%fused_computation.11 | convolution fusion | flops 2013265920 | bytes 9371648 | tf_op jit(solution)/shard_map/dot_general | solution.py:81
  165.0 0.4 convolution_convert_fusion.3
  165.4 2.3 fusion.11
  167.7 3.0 %fusion.1 = f32[640]{0:T(1024)S(1)} fusion(bf16[16,40,2048]{2,1,0:T(8,128)(2,1)} %all-to-all-done.1, f32[640,2048]{1,0:T(8,128)S(1)} %fusion.11, bf16[640,16]{0,1:T(8,128)(2,1)S(1)} %convolution_convert_fusion.3, bf16[1,16,2048]{2,1,0:T(8,128)(2,1)S(1)} %copy-done.6), kind=kOutput, calls=%fused_computation.5 | convolution fusion | flops 51117440 | bytes 7952896 | tf_op jit(solution)/shard_map/dot_general | solution.py:61
  170.7 0.7 all_to_all.23
  171.4 4.9 %all-to-all-start.4 = ((f32[16,1,40]{2,1,0:T(1,128)}), f32[16,1,40]{2,1,0:T(1,128)S(1)}, u32[]{:S(2)}, u32[]{:S(2)}) async-start(f32[16,1,40]{2,1,0:T(1,128)} %all_to_all.23), calls=%async_computation.4 | async-start | bytes 16384 | tf_op jit(solution)/shard_map/all_to_all | solution.py:177
  176.3 0.9 fusion.23
  177.2 6.8 %add_convert_fusion.1 = bf16[640,2048]{1,0:T(8,128)(2,1)} fusion(f32[640,2048]{1,0:T(8,128)S(1)} %fusion.23, f32[640,2048]{1,0:T(8,128)} %fusion.3, f32[640,2048]{1,0:T(8,128)} %fusion.7, bf16[640,16]{0,1:T(8,128)(2,1)S(1)} %convolution_convert_fusion.4, bf16[1,16,2048]{2,1,0:T(8,128)(2,1)S(1)} %copy-done.8), kind=kOutput, calls=%fused_computation.8 | convolution fusion | flops 48496640 | bytes 18436096 | tf_op jit(solution)/shard_map/dot_general | solution.py:89
  184.0 6.0 %all-to-all-start.3 = ((bf16[16,40,2048]{2,1,0:T(8,128)(2,1)}), bf16[16,40,2048]{2,1,0:T(8,128)(2,1)}, u32[]{:S(2)}, u32[]{:S(2)}) async-start(bf16[16,40,2048]{2,1,0:T(8,128)(2,1)} %bitcast.133), calls=%async_computation.3 | async-start | bytes 5242880 | tf_op jit(solution)/shard_map/all_to_all | solution.py:170
  190.1 0.1 reshape.151
  190.2 0.1 reshape.154
  190.3 2.1 fusion.20
  192.4 2.1 fusion.22
  194.4 2.1 fusion.21
  196.5 2.9 %fusion.16 = f32[1,16,2048]{2,1,0:T(8,128)} fusion(bf16[640,16]{0,1:T(8,128)(2,1)S(1)} %convolution_convert_fusion.4, bf16[640,2048]{1,0:T(8,128)(2,1)} %bitcast.8), kind=kOutput, calls=%fused_computation.27 | convolution fusion | flops 41975808 | bytes 2772992 | tf_op jit(solution)/shard_map/dot_general | solution.py:25
  199.4 2.9 %fusion.17 = f32[1,16,2048]{2,1,0:T(8,128)} fusion(bf16[640,16]{0,1:T(8,128)(2,1)S(1)} %convolution_convert_fusion.5, bf16[640,2048]{1,0:T(8,128)(2,1)} %bitcast.8), kind=kOutput, calls=%fused_computation.29 | convolution fusion | flops 41975808 | bytes 2772992 | tf_op jit(solution)/shard_map/dot_general | solution.py:25
  202.2 2.2 fusion.2
  204.5 1.1 fusion.15
  205.6 0.5 broadcast.103
  206.1 0.7 reduce.9
  206.8 0.1 reshape.150
  206.9 2.3 gather_fusion
  209.1 0.1 gather.7
  209.2 0.1 copy.61
  209.3 0.6 and_select_fusion
  209.9 38.9 %all-to-all-done.3 = bf16[16,40,2048]{2,1,0:T(8,128)(2,1)} async-done(((bf16[16,40,2048]{2,1,0:T(8,128)(2,1)}), bf16[16,40,2048]{2,1,0:T(8,128)(2,1)}, u32[]{:S(2)}, u32[]{:S(2)}) %all-to-all-start.3) | async-done | bytes 2621472 | tf_op jit(solution)/shard_map/all_to_all | solution.py:170
  248.8 3.0 %convolution_convert_fusion.2 = bf16[64,2048]{1,0:T(8,128)(2,1)} fusion(pred[640,64]{0,1:T(8,128)(4,1)S(1)} %fusion.19, bf16[640,2048]{1,0:T(8,128)(2,1)} %bitcast.16), kind=kOutput, calls=%fused_computation.23 | convolution fusion | flops 167903232 | bytes 2924544 | tf_op jit(solution)/shard_map/dot_general | solution.py:180
  (38 shorter events, 0.2 us)
Async XLA Ops:
  0.6 96.9 %copy-start = (bf16[1,2048,768]{2,1,0:T(8,128)(2,1)S(1)}, bf16[1,2048,768]{2,1,0:T(8,128)(2,1)}, u32[]{:S(2)}) copy-start(bf16[1,2048,768]{2,1,0:T(8,128)(2,1)} %param.18) | copy-start | bytes 9437188
  5.9 10.4 %all-to-all-start = ((bf16[16,1,40]{2,1,0:T(2,128)(2,1)}), bf16[16,1,40]{2,1,0:T(2,128)(2,1)S(1)}, u32[]{:S(2)}, u32[]{:S(2)}) async-start(bf16[16,1,40]{2,1,0:T(2,128)(2,1)} %convert_element_type.139), calls=%async_computation | async-start | bytes 16384 | tf_op jit(solution)/shard_map/all_to_all | solution.py:145
  16.3 7.0 %copy-start.5 = (bf16[64,2048]{1,0:T(8,128)(2,1)S(1)}, bf16[64,2048]{1,0:T(8,128)(2,1)}, u32[]{:S(2)}) copy-start(bf16[64,2048]{1,0:T(8,128)(2,1)} %param.14) | copy-start | bytes 786436
  16.3 65.7 %all-to-all-start.2 = ((bf16[16,40,2048]{2,1,0:T(8,128)(2,1)}), bf16[16,40,2048]{2,1,0:T(8,128)(2,1)}, u32[]{:S(2)}, u32[]{:S(2)}) async-start(bf16[16,40,2048]{2,1,0:T(8,128)(2,1)} %bitcast.130), calls=%async_computation.2 | async-start | bytes 5242880 | tf_op jit(solution)/shard_map/all_to_all | solution.py:131
  82.1 5.0 %copy-start.7 = (bf16[1,16,2048]{2,1,0:T(8,128)(2,1)S(1)}, bf16[1,16,2048]{2,1,0:T(8,128)(2,1)}, u32[]{:S(2)}) copy-start(bf16[1,16,2048]{2,1,0:T(8,128)(2,1)} %param.20) | copy-start | bytes 196612
  82.1 63.8 %all-to-all-start.1 = ((bf16[16,40,2048]{2,1,0:T(8,128)(2,1)}), bf16[16,40,2048]{2,1,0:T(8,128)(2,1)}, u32[]{:S(2)}, u32[]{:S(2)}) async-start(bf16[16,40,2048]{2,1,0:T(8,128)(2,1)} %bitcast.129), calls=%async_computation.1 | async-start | bytes 5242880 | tf_op jit(solution)/shard_map/all_to_all | solution.py:138
  87.1 2.7 %copy-start.8 = (bf16[1,16,2048]{2,1,0:T(8,128)(2,1)S(1)}, bf16[1,16,2048]{2,1,0:T(8,128)(2,1)}, u32[]{:S(2)}) copy-start(bf16[1,16,2048]{2,1,0:T(8,128)(2,1)} %param.22) | copy-start | bytes 196612
  87.1 5.2 %copy-start.12 = (bf16[1,2048,768]{2,1,0:T(8,128)(2,1)S(1)}, bf16[1,2048,768]{2,1,0:T(8,128)(2,1)}, u32[]{:S(2)}) copy-start(bf16[1,2048,768]{2,1,0:T(8,128)(2,1)} %param.17) | copy-start | bytes 9437188
  145.8 2.4 copy-start.6
  145.8 3.2 %copy-start.14 = (bf16[1,768,2048]{2,1,0:T(8,128)(2,1)S(1)}, bf16[1,768,2048]{2,1,0:T(8,128)(2,1)}, u32[]{:S(2)}) copy-start(bf16[1,768,2048]{2,1,0:T(8,128)(2,1)} %param.19) | copy-start | bytes 9437188
  149.0 2.3 copy-start.4
  149.0 2.3 copy-start.9
  151.3 0.7 copy-start.10
  152.0 0.7 copy-start.11
  152.0 1.6 copy-start.15
  154.9 5.0 %copy-start.1 = (bf16[640,768]{1,0:T(8,128)(2,1)}, bf16[640,768]{1,0:T(8,128)(2,1)S(1)}, u32[]{:S(2)}) copy-start(bf16[640,768]{1,0:T(8,128)(2,1)S(1)} %get-tuple-element.42) | copy-start | bytes 2949124
  154.9 5.4 %copy-start.2 = (bf16[640,768]{1,0:T(8,128)(2,1)}, bf16[640,768]{1,0:T(8,128)(2,1)S(1)}, u32[]{:S(2)}) copy-start(bf16[640,768]{1,0:T(8,128)(2,1)S(1)} %get-tuple-element.41) | copy-start | bytes 2949124
  154.9 10.5 %copy-start.3 = (bf16[640,768]{1,0:T(8,128)(2,1)}, bf16[640,768]{1,0:T(8,128)(2,1)S(1)}, u32[]{:S(2)}) copy-start(bf16[640,768]{1,0:T(8,128)(2,1)S(1)} %get-tuple-element.40) | copy-start | bytes 2949124
  155.3 5.0 %copy-start.13 = (bf16[1,2048,768]{2,1,0:T(8,128)(2,1)S(1)}, bf16[1,2048,768]{2,1,0:T(8,128)(2,1)}, u32[]{:S(2)}) copy-start(bf16[1,2048,768]{2,1,0:T(8,128)(2,1)} %param.17) | copy-start | bytes 9437188
  171.4 12.6 %all-to-all-start.4 = ((f32[16,1,40]{2,1,0:T(1,128)}), f32[16,1,40]{2,1,0:T(1,128)S(1)}, u32[]{:S(2)}, u32[]{:S(2)}) async-start(f32[16,1,40]{2,1,0:T(1,128)} %all_to_all.23), calls=%async_computation.4 | async-start | bytes 16384 | tf_op jit(solution)/shard_map/all_to_all | solution.py:177
  184.0 64.8 %all-to-all-start.3 = ((bf16[16,40,2048]{2,1,0:T(8,128)(2,1)}), bf16[16,40,2048]{2,1,0:T(8,128)(2,1)}, u32[]{:S(2)}, u32[]{:S(2)}) async-start(bf16[16,40,2048]{2,1,0:T(8,128)(2,1)} %bitcast.133), calls=%async_computation.3 | async-start | bytes 5242880 | tf_op jit(solution)/shard_map/all_to_all | solution.py:170
where the time goes:
time: 253 us; the launch traced here: 252 us
  waiting for transfers between devices  138 us (55%)
  matrix products  66.2 us (26%)
  starting transfers between devices  29.5 us (12%)
  other arithmetic  8.6 us (3%)
  local copies, waits for them, and re-layouts  8.36 us (3%)
    all_to_all x1, waiting for transfers between devices, shards(): lax.all_to_all(sent_rows.reshape(experts, capacity, features), 'expert',...  56.4 us
    all_to_all x1, waiting for transfers between devices, shards(): lax.all_to_all(sent_grads.reshape(experts, capacity, features), 'expert',...  43 us
    all_to_all x1, waiting for transfers between devices, shards(): lax.all_to_all(gradient_rows.reshape(peer_count, capacity, features), 'ex...  38.9 us
    dot_general x6, matrix products, outer_sum(): lax.dot_general(factor_matrix, multiplier, (((0,), (0,)), ((), ())), pref...  13 us
    dot_general x6, matrix products, low_rank(): lax.dot_general(factor_matrix, multiplier, (((1,), (1,)), ((), ())), pref...  7.06 us
    all_to_all x1, starting transfers between devices, shards(): lax.all_to_all(sent_rows.reshape(experts, capacity, features), 'expert',...  6.96 us
    dot_general x1, matrix products, expert_backward(): jnp.dot(up_reduced_gradient, up_adapter_input, preferred_element_type=jnp...  6.84 us
    all_to_all x1, starting transfers between devices, shards(): lax.all_to_all(slot_weight.reshape(experts, capacity), 'expert', split_ax...  6.55 us
  transfers between devices with their start and end apart: 5, of which 3 were waited for; matrix products, arithmetic and copies ran while one was open for 20% of the time, Pallas kernels for 0%

commit v1 on v0

--- a/solution.py
+++ b/solution.py
@@ -196,9 +196,42 @@
     )
 
 
+def gathered_shards(
+    tokens,
+    out_grad,
+    routes,
+    route_weights,
+    *expert_matrices,
+):
+    peer_count = lax.axis_size("expert")
+    tok_rows = tokens.shape[0]
+    experts = peer_count * expert_matrices[0].shape[0]
+    chosen = routes[:, :, None] == jnp.arange(experts, dtype=jnp.int32)[None, None, :]
+    weight_table = jnp.sum(
+        jnp.where(chosen, route_weights.astype(jnp.float32)[:, :, None], 0.0), 1
+    ).astype(jnp.bfloat16)
+    all_rows = lax.all_gather(tokens, "expert", axis=0, tiled=True)
+    all_grads = lax.all_gather(out_grad, "expert", axis=0, tiled=True)
+    all_weights = lax.all_gather(weight_table, "expert", axis=0, tiled=True)
+    own = jnp.arange(experts, dtype=jnp.int32)[None, :] == lax.axis_index("expert")
+    own_weight = jnp.sum(
+        jnp.where(own, all_weights.astype(jnp.float32), 0.0), 1
+    ).astype(jnp.bfloat16)
+    gradient_rows, expert_result, adapter_grads = expert_backward(
+        all_rows, all_grads, own_weight, *[matrix[0] for matrix in expert_matrices]
+    )
+    dots_here = jnp.sum(all_grads.astype(jnp.float32) * expert_result.astype(jnp.float32), -1)
+    grad_tokens = lax.psum_scatter(gradient_rows, "expert", scatter_dimension=0, tiled=True)
+    token_dots = lax.all_to_all(
+        dots_here.reshape(peer_count, tok_rows), "expert", split_axis=0, concat_axis=0, tiled=True
+    )
+    grad_weights = jnp.sum(jnp.where(chosen, token_dots.T[:, None, :], 0.0), 2)
+    return (grad_tokens, grad_weights) + tuple(grad[None] for grad in adapter_grads)
+
+
 def solution(mesh):
     return jax.shard_map(
-        shards,
+        gathered_shards if mesh.shape["expert"] <= 16 else shards,
         mesh=mesh,
         in_specs=(
             P(("groups", "expert"), None),

time: 253 us -> 261 us (1.032)
  the two profiles are of different devices: /device:TPU:15 before, /device:TPU:0 now
where the time goes in v1:
time: 261 us; the launch traced here: 260 us
  waiting for transfers between devices  149 us (57%)
  matrix products  68.2 us (26%)
  blocking collectives  17.7 us (7%)
  between operations  14 us (5%)
  local copies, waits for them, and re-layouts  6.11 us (2%)
  starting transfers between devices  3.77 us (1%)
    reduce_scatter x1, waiting for transfers between devices, gathered_shards(): lax.psum_scatter(gradient_rows, 'expert', scatter_dimension=0, tiled=True)  59.3 us
    all_gather x1, waiting for transfers between devices, gathered_shards(): all_rows = lax.all_gather(tokens, 'expert', axis=0, tiled=True)  54.8 us
    all_gather x1, waiting for transfers between devices, gathered_shards(): all_grads = lax.all_gather(out_grad, 'expert', axis=0, tiled=True)  27.4 us
    all_gather x1, blocking collectives, gathered_shards(): all_weights = lax.all_gather(weight_table, 'expert', axis=0, tiled=True)  17.7 us
    dot_general x6, matrix products, low_rank(): lax.dot_general(factor_matrix, multiplier, (((1,), (1,)), ((), ())), pref...  9.81 us
    dot_general x1, matrix products, expert_backward(): jnp.dot(up_reduced_gradient, up_adapter_input, preferred_element_type=jnp...  9 us
    dot_general x6, matrix products, outer_sum(): lax.dot_general(factor_matrix, multiplier, (((0,), (0,)), ((), ())), pref...  8.89 us
    dot_general x1, matrix products, expert_backward(): jnp.dot(hidden_reduced, down_adapter_output, preferred_element_type=jnp.f...  6.28 us
  transfers between devices with their start and end apart: 4, of which 4 were waited for; matrix products, arithmetic and copies ran while one was open for 12% of the time, Pallas kernels for 0%

profile of v1, /device:TPU:0, one launch (start us, length us, event | category | flops | bytes accessed | tf_op | source)
XLA Modules:
  0.0 260.3 jit_solution(421264079084392577)
XLA Ops:
  7.2 0.0 copy-start
  7.2 0.0 copy-start.12
  7.2 0.0 all-gather.6.cloned.1.call-start
  7.2 0.7 all-gather.6.cloned.1.call-update
  7.9 0.0 all-gather.4.cloned.1.call-start
  8.0 0.7 all-gather.4.cloned.1.call-update
  8.7 54.8 %all-gather.6.cloned.1.call-done = bf16[1024,2048]{1,0:T(8,128)(2,1)} async-done(((bf16[64,2048]{1,0:T(8,128)(2,1)}), bf16[1024,2048]{1,0:T(8,128)(2,1)}) %all-gather.6.cloned.1.call-update) | async-done | bytes 4194320 | tf_op jit(solution)/shard_map/all_gather | solution.py:213
  63.5 3.5 %convolution_convert_fusion.3 = bf16[1024,16]{0,1:T(8,128)(2,1)S(1)} fusion(bf16[1024,2048]{1,0:T(8,128)(2,1)} %all-gather.6.cloned.1.call-done, bf16[1,16,2048]{2,1,0:T(8,128)(2,1)} %param.20), kind=kOutput, calls=%fused_computation.41 | convolution fusion | flops 67125248 | bytes 4292608 | tf_op jit(solution)/shard_map/dot_general | solution.py:19
  67.0 0.0 copy-done.12
  67.0 0.0 copy-done.2
  67.0 0.0 copy-start.20
  67.0 1.2 convolution_convert_fusion.4
  68.2 0.7 copy-done.20
  68.9 3.4 %fusion.4 = f32[1024,768]{1,0:T(8,128)S(1)} fusion(bf16[1024,2048]{1,0:T(8,128)(2,1)S(1)} %copy-done.2, bf16[1,2048,768]{2,1,0:T(8,128)(2,1)S(1)} %copy-done.20), kind=kOutput, calls=%fused_computation.8 | convolution fusion | flops 3221225472 | bytes 10485760 | tf_op jit(solution)/shard_map/dot_general | solution.py:46
  72.4 0.0 copy-done.13
  72.4 0.0 copy-start.22
  72.4 0.6 multiply_add_fusion
  73.0 1.3 copy-done.22
  74.3 3.4 %fusion.8 = f32[1024,768]{1,0:T(8,128)S(1)} fusion(bf16[1024,2048]{1,0:T(8,128)(2,1)S(1)} %copy-done.2, bf16[1,2048,768]{2,1,0:T(8,128)(2,1)S(1)} %copy-done.22), kind=kOutput, calls=%fused_computation.12 | convolution fusion | flops 3221225472 | bytes 10485760 | tf_op jit(solution)/shard_map/dot_general | solution.py:51
  77.7 0.0 copy-done.9
  77.7 0.0 copy-done.16
  77.7 0.0 copy-start.15
  77.8 2.9 %multiply_convert_fusion = (bf16[1024,768]{1,0:T(8,128)(2,1)S(1)}, f32[1024,768]{1,0:T(8,128)}) fusion(f32[1024,768]{1,0:T(8,128)S(1)} %multiply_add_fusion, f32[1024,768]{1,0:T(8,128)S(1)} %fusion.8, bf16[1024,16]{0,1:T(8,128)(2,1)S(1)} %convolution_convert_fusion.4, bf16[1,16,768]{2,1,0:T(8,128)(2,1)S(1)} %copy-done.16), kind=kOutput, calls=%fused_computation.18 | convolution fusion | flops 31457280 | bytes 11067392 | tf_op jit(solution)/shard_map/dot_general | solution.py:53
  80.6 0.0 copy-done.15
  80.6 0.5 convolution_convert_fusion
  81.1 0.7 copy-done.6
  81.8 0.0 copy-done
  81.8 5.7 %fusion.10 = f32[1024,2048]{1,0:T(8,128)} fusion(bf16[1024,768]{1,0:T(8,128)(2,1)S(1)} %get-tuple-element.12, bf16[1,768,2048]{2,1,0:T(8,128)(2,1)S(1)} %copy-done), kind=kOutput, calls=%fused_computation.14 | convolution fusion | flops 3221225472 | bytes 13107200 | tf_op jit(solution)/shard_map/dot_general | solution.py:59
  87.5 27.4 %all-gather.4.cloned.1.call-done = bf16[1024,2048]{1,0:T(8,128)(2,1)} async-done(((bf16[64,2048]{1,0:T(8,128)(2,1)}), bf16[1024,2048]{1,0:T(8,128)(2,1)}) %all-gather.4.cloned.1.call-update) | async-done | bytes 4194320 | tf_op jit(solution)/shard_map/all_gather | solution.py:214
  114.9 0.0 copy-done.14
  114.9 6.3 %fusion.1 = f32[1024]{0:T(1024)S(1)} fusion(bf16[1024,2048]{1,0:T(8,128)(2,1)} %all-gather.4.cloned.1.call-done, f32[1024,2048]{1,0:T(8,128)} %fusion.10, bf16[1024,16]{0,1:T(8,128)(2,1)S(1)} %convolution_convert_fusion, bf16[1,16,2048]{2,1,0:T(8,128)(2,1)S(1)} %copy-done.14), kind=kOutput, calls=%fused_computation.3 | convolution fusion | flops 81787904 | bytes 12685312 | tf_op jit(solution)/shard_map/dot_general | solution.py:61
  121.2 0.7 all_to_all.8
  121.9 3.7 %all-to-all-start = ((f32[16,1,64]{2,1,0:T(1,128)}), f32[16,1,64]{2,1,0:T(1,128)S(1)}, u32[]{:S(2)}, u32[]{:S(2)}) async-start(f32[16,1,64]{2,1,0:T(1,128)} %bitcast.10), calls=%async_computation.1 | async-start | bytes 16384 | tf_op jit(solution)/shard_map/all_to_all | solution.py:225
  125.5 0.0 reduce-scatter.2.cloned.1.call-start
  125.6 0.5 iota_compare_fusion.1
  126.1 5.7 %all-to-all-done = f32[16,1,64]{2,1,0:T(1,128)S(1)} async-done(((f32[16,1,64]{2,1,0:T(1,128)}), f32[16,1,64]{2,1,0:T(1,128)S(1)}, u32[]{:S(2)}, u32[]{:S(2)}) %all-to-all-start) | async-done | bytes 4128 | tf_op jit(solution)/shard_map/all_to_all | solution.py:225
  131.8 0.6 select_reduce_fusion
  132.4 17.7 %all-gather = bf16[16,64,16]{1,2,0:T(8,128)(2,1)S(1)} all-gather(bf16[1,64,16]{1,2,0:T(8,128)(2,1)S(1)} %bitcast.98), channel_id=1, replica_groups=mesh['groups'=2,'expert'=16] {'expert'}, dimensions={0}, use_global_device_ids=true | all-gather | bytes 34816 | tf_op jit(solution)/shard_map/all_gather | solution.py:215
  150.2 0.1 reshape.34
  150.3 0.7 select_reduce_fusion.1
  151.1 3.6 %convolution_convert_fusion.5 = bf16[1024,16]{0,1:T(8,128)(2,1)S(1)} fusion(bf16[1,16,2048]{2,1,0:T(8,128)(2,1)} %param.25, bf16[1024,2048]{1,0:T(8,128)(2,1)} %all-gather.4.cloned.1.call-done, f32[1024]{0:T(1024)S(1)} %convert_element_type.116), kind=kOutput, calls=%fused_computation.43 | convolution fusion | flops 73416704 | bytes 4296704 | tf_op jit(solution)/shard_map/dot_general | solution.py:19
  154.6 0.0 copy-start.24
  154.7 3.5 %fusion.12 = f32[1024,768]{1,0:T(8,128)S(1)} fusion(bf16[1,768,2048]{2,1,0:T(8,128)(2,1)S(1)} %copy-done, bf16[1024,2048]{1,0:T(8,128)(2,1)S(1)} %copy-done.4, f32[1024]{0:T(1024)S(1)} %convert_element_type.116), kind=kOutput, calls=%fused_computation.16 | convolution fusion | flops 3227516928 | bytes 10489856 | tf_op jit(solution)/shard_map/dot_general | solution.py:67
  158.2 0.0 copy-start.21
  158.2 1.9 multiply_convert_fusion.1
  160.1 0.5 convolution_convert_fusion.2
  160.7 0.0 copy-start.23
  160.7 5.8 %fusion.2 = f32[1024,2048]{1,0:T(8,128)} fusion(bf16[1024,768]{1,0:T(8,128)(2,1)S(1)} %get-tuple-element.11, bf16[1,2048,768]{2,1,0:T(8,128)(2,1)S(1)} %copy-done.21), kind=kOutput, calls=%fused_computation.6 | convolution fusion | flops 3221225472 | bytes 13107200 | tf_op jit(solution)/shard_map/dot_general | solution.py:81
  166.4 0.5 convolution_convert_fusion.1
  167.0 0.0 copy-start.11
  167.0 5.8 %fusion.6 = f32[1024,2048]{1,0:T(8,128)} fusion(bf16[1024,768]{1,0:T(8,128)(2,1)S(1)} %get-tuple-element.10, bf16[1,2048,768]{2,1,0:T(8,128)(2,1)S(1)} %copy-done.23), kind=kOutput, calls=%fused_computation.10 | convolution fusion | flops 3221225472 | bytes 13107200 | tf_op jit(solution)/shard_map/dot_general | solution.py:84
  172.7 1.3 fusion.21
  174.0 9.0 %add_convert_fusion.1 = bf16[1024,2048]{1,0:T(8,128)(2,1)} fusion(f32[1024,2048]{1,0:T(8,128)S(1)} %fusion.21, f32[1024,2048]{1,0:T(8,128)} %fusion.2, f32[1024,2048]{1,0:T(8,128)} %fusion.6, bf16[1024,16]{0,1:T(8,128)(2,1)S(1)} %convolution_convert_fusion.1, bf16[1,16,2048]{2,1,0:T(8,128)(2,1)S(1)} %copy-done.12), kind=kOutput, calls=%fused_computation.5 | convolution fusion | flops 77594624 | bytes 29458432 | tf_op jit(solution)/shard_map/dot_general | solution.py:89
  183.0 0.0 reduce-scatter.2.cloned.1.call-update
  183.0 1.4 copy-done.7
  184.4 0.9 fusion.18
  185.4 2.8 %fusion.19 = f32[1,16,768]{2,1,0:T(8,128)} fusion(bf16[1024,16]{0,1:T(8,128)(2,1)S(1)} %convolution_convert_fusion.4, bf16[1024,768]{1,0:T(8,128)(2,1)} %copy-done.8), kind=kOutput, calls=%fused_computation.38 | convolution fusion | flops 25178112 | bytes 1654784 | tf_op jit(solution)/shard_map/dot_general | solution.py:25
  188.2 0.9 fusion.20
  189.1 1.3 fusion.17
  190.5 1.3 fusion.16
  191.8 1.1 copy-done.5
  192.9 1.5 fusion.15
  194.5 59.3 %reduce-scatter.2.cloned.1.call-done = bf16[64,2048]{1,0:T(8,128)(2,1)} async-done(((bf16[1024,2048]{1,0:T(8,128)(2,1)}), bf16[64,2048]{1,0:T(8,128)(2,1)}) %reduce-scatter.2.cloned.1.call-update) | async-done | bytes 262160 | tf_op jit(solution)/shard_map/reduce_scatter | solution.py:224
  253.8 0.0 copy-done.1
  (30 shorter events, 0.1 us)
Async XLA Ops:
  7.2 74.6 %copy-start = (bf16[1,768,2048]{2,1,0:T(8,128)(2,1)S(1)}, bf16[1,768,2048]{2,1,0:T(8,128)(2,1)}, u32[]{:S(2)}) copy-start(bf16[1,768,2048]{2,1,0:T(8,128)(2,1)} %param.19) | copy-start | bytes 9437188
  7.2 59.8 %copy-start.12 = (bf16[1,16,2048]{2,1,0:T(8,128)(2,1)S(1)}, bf16[1,16,2048]{2,1,0:T(8,128)(2,1)}, u32[]{:S(2)}) copy-start(bf16[1,16,2048]{2,1,0:T(8,128)(2,1)} %param.22) | copy-start | bytes 196612
  7.2 56.3 %all-gather.6.cloned.1.call-start = ((), (), s32[]{:S(2)}) async-start(), calls=%async_computation.3 | async-start | bytes 4456448 | tf_op jit(solution)/shard_map/all_gather | solution.py:213
  7.9 107.0 %all-gather.4.cloned.1.call-start = ((), (), s32[]{:S(2)}) async-start(), calls=%async_computation.2 | async-start | bytes 4456448 | tf_op jit(solution)/shard_map/all_gather | solution.py:214
  63.5 3.5 %copy-start.2 = (bf16[1024,2048]{1,0:T(8,128)(2,1)S(1)}, bf16[1024,2048]{1,0:T(8,128)(2,1)}, u32[]{:S(2)}) copy-start(bf16[1024,2048]{1,0:T(8,128)(2,1)} %all-gather.6.cloned.1.call-done) | copy-start | bytes 12582916
  67.0 1.9 copy-start.20
  68.9 3.4 %copy-start.13 = (bf16[1,16,768]{2,1,0:T(8,128)(2,1)S(1)}, bf16[1,16,768]{2,1,0:T(8,128)(2,1)}, u32[]{:S(2)}) copy-start(bf16[1,16,768]{2,1,0:T(8,128)(2,1)} %param.21) | copy-start | bytes 73732
  72.4 1.9 copy-start.22
  74.3 3.4 %copy-start.9 = (f32[1024,768]{1,0:T(8,128)}, f32[1024,768]{1,0:T(8,128)S(1)}, u32[]{:S(2)}) copy-start(f32[1024,768]{1,0:T(8,128)S(1)} %multiply_add_fusion) | copy-start | bytes 9437188
  74.3 3.4 %copy-start.16 = (bf16[1,16,768]{2,1,0:T(8,128)(2,1)S(1)}, bf16[1,16,768]{2,1,0:T(8,128)(2,1)}, u32[]{:S(2)}) copy-start(bf16[1,16,768]{2,1,0:T(8,128)(2,1)} %param.23) | copy-start | bytes 73732
  77.7 2.9 %copy-start.15 = (bf16[1,16,768]{2,1,0:T(8,128)(2,1)S(1)}, bf16[1,16,768]{2,1,0:T(8,128)(2,1)}, u32[]{:S(2)}) copy-start(bf16[1,16,768]{2,1,0:T(8,128)(2,1)} %param.24) | copy-start | bytes 73732
  80.6 1.2 copy-start.6
  81.8 33.1 %copy-start.14 = (bf16[1,16,2048]{2,1,0:T(8,128)(2,1)S(1)}, bf16[1,16,2048]{2,1,0:T(8,128)(2,1)}, u32[]{:S(2)}) copy-start(bf16[1,16,2048]{2,1,0:T(8,128)(2,1)} %param.25) | copy-start | bytes 196612
  87.5 38.6 %copy-start.19 = (bf16[64,8]{0,1:T(8,128)(2,1)S(1)}, bf16[64,8]{0,1:T(8,128)(2,1)}, u32[]{:S(2)}) copy-start(bf16[64,8]{0,1:T(8,128)(2,1)} %param.16) | copy-start | bytes 3076
  87.5 44.3 %copy-start.18 = (s32[64,8]{0,1:T(8,128)S(1)}, s32[64,8]{0,1:T(8,128)}, u32[]{:S(2)}) copy-start(s32[64,8]{0,1:T(8,128)} %param.15) | copy-start | bytes 6148
  121.9 10.0 %all-to-all-start = ((f32[16,1,64]{2,1,0:T(1,128)}), f32[16,1,64]{2,1,0:T(1,128)S(1)}, u32[]{:S(2)}, u32[]{:S(2)}) async-start(f32[16,1,64]{2,1,0:T(1,128)} %bitcast.10), calls=%async_computation.1 | async-start | bytes 16384 | tf_op jit(solution)/shard_map/all_to_all | solution.py:225
  125.5 128.3 %reduce-scatter.2.cloned.1.call-start = ((), (), s32[]{:S(2)}) async-start(), calls=%async_computation.4 | async-start | bytes 4456448 | tf_op jit(solution)/shard_map/reduce_scatter | solution.py:224
  151.0 3.6 %copy-start.4 = (bf16[1024,2048]{1,0:T(8,128)(2,1)S(1)}, bf16[1024,2048]{1,0:T(8,128)(2,1)}, u32[]{:S(2)}) copy-start(bf16[1024,2048]{1,0:T(8,128)(2,1)} %all-gather.4.cloned.1.call-done) | copy-start | bytes 12582916
  154.6 3.5 %copy-start.10 = (f32[1024,768]{1,0:T(8,128)S(1)}, f32[1024,768]{1,0:T(8,128)}, u32[]{:S(2)}) copy-start(f32[1024,768]{1,0:T(8,128)} %copy-done.9) | copy-start | bytes 9437188
  154.6 3.5 %copy-start.24 = (f32[1024,768]{1,0:T(8,128)S(1)}, f32[1024,768]{1,0:T(8,128)}, u32[]{:S(2)}) copy-start(f32[1024,768]{1,0:T(8,128)} %get-tuple-element.13) | copy-start | bytes 9437188
  158.2 2.5 copy-start.21
  160.1 6.8 %copy-start.8 = (bf16[1024,768]{1,0:T(8,128)(2,1)}, bf16[1024,768]{1,0:T(8,128)(2,1)S(1)}, u32[]{:S(2)}) copy-start(bf16[1024,768]{1,0:T(8,128)(2,1)S(1)} %get-tuple-element.10) | copy-start | bytes 4718596
  160.6 5.8 %copy-start.17 = (bf16[1,16,768]{2,1,0:T(8,128)(2,1)S(1)}, bf16[1,16,768]{2,1,0:T(8,128)(2,1)}, u32[]{:S(2)}) copy-start(bf16[1,16,768]{2,1,0:T(8,128)(2,1)} %param.23) | copy-start | bytes 73732
  160.7 6.3 %copy-start.23 = (bf16[1,2048,768]{2,1,0:T(8,128)(2,1)S(1)}, bf16[1,2048,768]{2,1,0:T(8,128)(2,1)}, u32[]{:S(2)}) copy-start(bf16[1,2048,768]{2,1,0:T(8,128)(2,1)} %param.18) | copy-start | bytes 9437188
  167.0 5.8 %copy-start.11 = (bf16[1,16,2048]{2,1,0:T(8,128)(2,1)S(1)}, bf16[1,16,2048]{2,1,0:T(8,128)(2,1)}, u32[]{:S(2)}) copy-start(bf16[1,16,2048]{2,1,0:T(8,128)(2,1)} %param.20) | copy-start | bytes 196612
  183.0 1.4 copy-start.7
  184.4 4.7 %copy-start.3 = (bf16[1024,2048]{1,0:T(8,128)(2,1)S(1)}, bf16[1024,2048]{1,0:T(8,128)(2,1)}, u32[]{:S(2)}) copy-start(bf16[1024,2048]{1,0:T(8,128)(2,1)} %all-gather.6.cloned.1.call-done) | copy-start | bytes 12582916
  190.5 2.5 copy-start.5
  190.5 63.3 %copy-start.1 = (bf16[1,768,2048]{2,1,0:T(8,128)(2,1)S(1)}, bf16[1,768,2048]{2,1,0:T(8,128)(2,1)}, u32[]{:S(2)}) copy-start(bf16[1,768,2048]{2,1,0:T(8,128)(2,1)} %param.19) | copy-start | bytes 9437188
Sparse Core Ops, SparseCore 0:
  10.2 53.2 all-gather.5
  65.6 49.2 all-gather.3
  183.2 70.5 reduce-scatter.1

commit v2 on v0

--- a/solution.py
+++ b/solution.py
@@ -1,9 +1,448 @@
 import jax
 import jax.numpy as jnp
 from jax import lax
+from jax.experimental import pallas as pl
+from jax.experimental.pallas import tpu as pltpu
 from jax.sharding import PartitionSpec as P
 
 ADAPTER_SCALING = 0.5
+LANES = 128
+PIECES = 4
+SIB, SIDE, UP, DOWN = 0, 1, 2, 3
+F32, BF16 = jnp.float32, jnp.bfloat16
+
+
+def mm(a, b):
+    return jnp.dot(a, b, preferred_element_type=F32)
+
+
+def mm_t(a, b):
+    return lax.dot_general(a, b, (((1,), (1,)), ((), ())), preferred_element_type=F32)
+
+
+def turned(value):
+    return value.astype(F32).T.astype(BF16)
+
+
+def routed_kernel(
+    x_ref, g_ref, routes_ref, weights_ref, wg, wu, wd, gin, gout, uin, uout, din, dout,
+    tok_out, rw_out, ag_out, bg_out, au_out, bu_out, ad_out, bd_out,
+    xbuf, gbuf, part, sbuf, ybuf, zbuf,
+    ain, aout, dinp, doutp, gate_s, up_s, gh_s, hid_s, gg_s, gu_s, low_s, hlow_s, wcol_s,
+    acc_a, acc_b, acc_ad, acc_bd, total_s,
+    xs, xr, gs, gr, ss, sr, ys, yr, zs, zr,
+):
+    rows, feat = x_ref.shape
+    rank, hid = gout.shape
+    plane_rows = 4 * rows
+    piece = rows // PIECES
+    me = lax.axis_index("expert")
+    z, y, c = me // 4, (me // 2) % 2, me % 2
+    half = z // 2
+    inner = (z % 3 + 1) // 2
+    target = {SIB: me + 1 - 2 * c, SIDE: me + 2 - 4 * y, UP: (me + 4) % 16, DOWN: (me + 12) % 16}
+
+    def plane_at(s):
+        p = s + inner * (1 - s // 2) * (1 - 2 * s)
+        return p + half * (3 - 2 * p)
+
+    def block(p, yy, cc):
+        return p * 4 + yy * 2 + cc
+
+    def remote(src, dst, send, recv, kind):
+        return pltpu.make_async_remote_copy(
+            src_ref=src, dst_ref=dst, send_sem=send, recv_sem=recv,
+            device_id={"expert": target[kind]}, device_id_type=pl.DeviceIdType.MESH,
+        )
+
+    barrier = pltpu.get_barrier_semaphore()
+
+    def greet(kind):
+        pl.semaphore_signal(
+            barrier, inc=1, device_id={"expert": target[kind]},
+            device_id_type=pl.DeviceIdType.MESH,
+        )
+
+    greet(SIB)
+    greet(SIDE)
+    pl.when(z < 3)(lambda: greet(UP))
+    pl.when(z > 0)(lambda: greet(DOWN))
+
+    own = pl.ds(me * rows, rows)
+    xbuf[own, :] = x_ref[...]
+    gbuf[own, 0:feat] = g_ref[...]
+    lane = lax.broadcasted_iota(jnp.int32, (rows, LANES), 1)
+    route = routes_ref[...]
+    route_w = weights_ref[...].astype(F32)
+    table = jnp.zeros((rows, LANES), F32)
+    for k in range(route.shape[1]):
+        table = jnp.where(lane == route[:, k : k + 1], route_w[:, k : k + 1], table)
+    gbuf[own, feat:] = table.astype(BF16)
+
+    pl.semaphore_wait(barrier, 3 + inner)
+
+    def wide(buf, send, recv, kind, b):
+        at = buf.at[pl.ds(b * rows, rows)]
+        return remote(at, at, send.at[kind, b], recv.at[b], kind)
+
+    arrays = ((xbuf, xs, xr), (gbuf, gs, gr))
+
+    def each_own(arr, act):
+        act(wide(*arr, SIDE, me))
+        pl.when(z < 3)(lambda: act(wide(*arr, UP, me)))
+        pl.when(z > 0)(lambda: act(wide(*arr, DOWN, me)))
+        act(wide(*arr, SIB, me))
+
+    def each_column(arr, p, act):
+        b = block(p, y, c)
+        pl.when(jnp.logical_and(p < z, z < 3))(lambda: act(wide(*arr, UP, b)))
+        pl.when(jnp.logical_and(p > z, z > 0))(lambda: act(wide(*arr, DOWN, b)))
+        act(wide(*arr, SIDE, b))
+        act(wide(*arr, SIB, b))
+
+    def start(copy):
+        copy.start()
+
+    def relay_z(arr, p):
+        wide(*arr, SIB, block(p, y, c)).wait_recv()
+        each_column(arr, p, start)
+
+    def relay_y(arr, p):
+        b = block(p, 1 - y, c)
+        wide(*arr, SIB, b).wait_recv()
+        wide(*arr, SIB, b).start()
+
+    def wait_sib(arr, p):
+        wide(*arr, SIB, block(p, 0, 1 - c)).wait_recv()
+        wide(*arr, SIB, block(p, 1, 1 - c)).wait_recv()
+
+    def relays(arr, s):
+        relay_y(arr, plane_at(s))
+
+        @pl.when(s < 3 - inner)
+        def _():
+            relay_z(arr, plane_at(s + 1 + inner * s))
+
+        @pl.when(jnp.logical_and(inner == 1, s == 0))
+        def _():
+            relay_z(arr, plane_at(2))
+
+    for arr in arrays:
+        each_own(arr, start)
+
+    ain[...] = jnp.zeros_like(ain)
+    aout[...] = jnp.zeros_like(aout)
+    dinp[...] = jnp.zeros_like(dinp)
+    doutp[...] = jnp.zeros_like(doutp)
+    ain[0:rank, :] = gin[...]
+    ain[rank : 2 * rank, :] = uin[...]
+    aout[0:rank, 0:hid] = gout[...]
+    aout[rank : 2 * rank, hid:] = uout[...]
+    dinp[0:rank, :] = din[...]
+    doutp[0:rank, :] = dout[...]
+    acc_a[...] = jnp.zeros_like(acc_a)
+    acc_b[...] = jnp.zeros_like(acc_b)
+    acc_ad[...] = jnp.zeros_like(acc_ad)
+    acc_bd[...] = jnp.zeros_like(acc_bd)
+
+    def to_sib(p, yy):
+        return remote(
+            part.at[pl.ds(block(p, yy, 1 - c) * rows, rows)],
+            sbuf.at[pl.ds((p * 2 + yy) * rows, rows)],
+            ss.at[p * 2 + yy], sr.at[p * 2 + yy], SIB,
+        )
+
+    def to_side(p, h):
+        return remote(
+            sbuf.at[pl.ds((p * 2 + 1 - y) * rows + h * piece, piece)],
+            ybuf.at[pl.ds(p * rows + h * piece, piece)],
+            ys.at[p, h], yr.at[p, h], SIDE,
+        )
+
+    def along(p, h, kind):
+        lead = 0 if kind == UP else 1
+        return remote(
+            ybuf.at[pl.ds(p * rows + h * piece, piece)],
+            zbuf.at[lead, pl.ds(p * rows + h * piece, piece)],
+            zs.at[p, h], zr.at[lead, p, h], kind,
+        )
+
+    def sum_sib(p):
+        to_sib(p, 1 - y).wait_recv()
+
+        def step(h, _):
+            at = pl.ds((p * 2 + 1 - y) * rows + h * piece, piece)
+            mine = pl.ds(block(p, 1 - y, c) * rows + h * piece, piece)
+            sbuf[at, :] = (sbuf[at, :].astype(F32) + part[mine, :].astype(F32)).astype(BF16)
+            to_side(p, h).start()
+            return 0
+
+        lax.fori_loop(0, PIECES, step, 0)
+        to_sib(p, y).wait_recv()
+
+    def pair_sum(p, h):
+        to_side(p, h).wait_recv()
+        here = pl.ds(block(p, y, c) * rows + h * piece, piece)
+        near = pl.ds((p * 2 + y) * rows + h * piece, piece)
+        at = pl.ds(p * rows + h * piece, piece)
+        return part[here, :].astype(F32) + sbuf[near, :].astype(F32) + ybuf[at, :].astype(F32)
+
+    def pass_on(p, h):
+        at = pl.ds(p * rows + h * piece, piece)
+        ybuf[at, :] = pair_sum(p, h).astype(BF16)
+
+        @pl.when(p > z)
+        def _():
+            @pl.when(z > 0)
+            def _():
+                along(p, h, UP).wait_recv()
+                ybuf[at, :] = (ybuf[at, :].astype(F32) + zbuf[0, at, :].astype(F32)).astype(BF16)
+
+            along(p, h, UP).start()
+
+        @pl.when(p < z)
+        def _():
+            @pl.when(z < 3)
+            def _():
+                along(p, h, DOWN).wait_recv()
+                ybuf[at, :] = (ybuf[at, :].astype(F32) + zbuf[1, at, :].astype(F32)).astype(BF16)
+
+            along(p, h, DOWN).start()
+
+    def pass_all(p):
+        def step(h, _):
+            pass_on(p, h)
+            return 0
+
+        lax.fori_loop(0, PIECES, step, 0)
+
+    chunk = 16
+    expert_lane = lax.broadcasted_iota(jnp.int32, (chunk, LANES), 1)
+
+    def forward(p):
+        at = pl.ds(p * plane_rows, plane_rows)
+        x = xbuf[at, :]
+        low = mm_t(x, ain[...]).astype(BF16)
+        low_s[...] = low
+        gate_s[...] = mm(x, wg[...]) + ADAPTER_SCALING * mm(low, aout[:, 0:hid])
+        up_s[...] = mm(x, wu[...]) + ADAPTER_SCALING * mm(low, aout[:, hid:])
+
+        def step(r, _):
+            rr = pl.ds(r * chunk, chunk)
+            gate = gate_s[rr, :]
+            act = gate * jax.nn.sigmoid(gate)
+            hid_s[rr, :] = (act * up_s[rr, :]).astype(BF16)
+            return 0
+
+        lax.fori_loop(0, plane_rows // chunk, step, 0)
+        hlow_s[...] = mm_t(hid_s[...], dinp[...])
+
+    def backward(p):
+        at = pl.ds(p * plane_rows, plane_rows)
+        g = gbuf[at, 0:feat]
+        glow = mm_t(g, doutp[...])
+        gh_s[...] = mm_t(g, wd[...]) + ADAPTER_SCALING * mm(glow.astype(BF16), dinp[...])
+
+        def step(r, _):
+            rr = pl.ds(r * chunk, chunk)
+            full = pl.ds(p * plane_rows + r * chunk, chunk)
+            gh = gh_s[rr, :]
+            gate = gate_s[rr, :]
+            up = up_s[rr, :]
+            sig = jax.nn.sigmoid(gate)
+            act = gate * sig
+            w = jnp.sum(
+                jnp.where(expert_lane == me, gbuf[full, feat:].astype(F32), 0.0), 1, keepdims=True
+            )
+            wcol_s[rr, :] = jnp.broadcast_to(w, (chunk, LANES))
+            dots = jnp.sum(hid_s[rr, :].astype(F32) * gh, 1, keepdims=True)
+            high = dots.astype(BF16).astype(F32)
+            part[full, feat:] = jnp.where(
+                expert_lane == me, high, jnp.where(expert_lane == me + 16, dots - high, 0.0)
+            ).astype(BF16)
+            gh = gh * w
+            gg_s[rr, :] = (gh * up * sig * (1.0 + gate * (1.0 - sig))).astype(BF16)
+            gu_s[rr, :] = (gh * act).astype(BF16)
+            return 0
+
+        lax.fori_loop(0, plane_rows // chunk, step, 0)
+        gg, gu = gg_s[...], gu_s[...]
+        lg = (mm_t(gg, aout[:, 0:hid]) + mm_t(gu, aout[:, hid:])).astype(BF16)
+        wide_n = min(512, feat)
+        for n in range(0, feat, wide_n):
+            cols = slice(n, n + wide_n)
+            part[at, cols] = (
+                mm_t(gg, wg[cols, :])
+                + mm_t(gu, wu[cols, :])
+                + ADAPTER_SCALING * mm(lg, ain[:, cols])
+            ).astype(BF16)
+        return glow, lg
+
+    def outer(p, glow, lg):
+        at = pl.ds(p * plane_rows, plane_rows)
+        w = wcol_s[...]
+        acc_a[...] += mm(turned(lg)[0 : 2 * rank], xbuf[at, :])
+        low_t = turned(low_s[...])[0 : 2 * rank]
+        acc_b[:, 0:hid] += mm(low_t, gg_s[...])
+        acc_b[:, hid:] += mm(low_t, gu_s[...])
+        acc_ad[...] += mm(turned(w * glow)[0:rank], hid_s[...])
+        hlow = hlow_s[...].astype(BF16).astype(F32)
+        acc_bd[...] += mm(turned(w * hlow)[0:rank], gbuf[at, 0:feat])
+
+    def body(s, _):
+        p = plane_at(s)
+        before = plane_at(jnp.maximum(s - 1, 0))
+        relays(arrays[0], s)
+        wait_sib(arrays[0], p)
+        forward(p)
+        pl.when(s >= 1)(lambda: sum_sib(before))
+        relays(arrays[1], s)
+        wait_sib(arrays[1], p)
+        glow, lg = backward(p)
+        to_sib(p, 0).start()
+        to_sib(p, 1).start()
+        outer(p, glow, lg)
+        pl.when(s >= 2 + inner)(lambda: pass_all(before))
+        return 0
+
+    lax.fori_loop(0, 4, body, 0)
+    last = plane_at(3)
+    sum_sib(last)
+
+    def tail(h, _):
+        pass_on(last, h)
+        pl.when(inner == 1)(lambda: pass_on(plane_at(1), h))
+        return 0
+
+    lax.fori_loop(0, PIECES, tail, 0)
+
+    ag_out[...] = ADAPTER_SCALING * acc_a[0:rank, :]
+    au_out[...] = ADAPTER_SCALING * acc_a[rank : 2 * rank, :]
+    bg_out[...] = ADAPTER_SCALING * acc_b[0:rank, 0:hid]
+    bu_out[...] = ADAPTER_SCALING * acc_b[rank : 2 * rank, hid:]
+    ad_out[...] = ADAPTER_SCALING * acc_ad[...]
+    bd_out[...] = ADAPTER_SCALING * acc_bd[...]
+
+    def finish(h, _):
+        at = pl.ds(z * rows + h * piece, piece)
+        total_s[...] = pair_sum(z, h)
+
+        @pl.when(z > 0)
+        def _():
+            along(z, h, UP).wait_recv()
+            total_s[...] += zbuf[0, at, :].astype(F32)
+
+        @pl.when(z < 3)
+        def _():
+            along(z, h, DOWN).wait_recv()
+            total_s[...] += zbuf[1, at, :].astype(F32)
+
+        ybuf[at, :] = total_s[...].astype(BF16)
+        return 0
+
+    lax.fori_loop(0, PIECES, finish, 0)
+    at = pl.ds(z * rows, rows)
+    tok_out[...] = ybuf[at, 0:feat]
+    dots = ybuf[at, feat:].astype(F32)
+    place = lax.broadcasted_iota(jnp.int32, route.shape, 1)
+    result = jnp.zeros(route.shape, F32)
+    for k in range(route.shape[1]):
+        pick = jnp.logical_or(lane == route[:, k : k + 1], lane == route[:, k : k + 1] + 16)
+        value = jnp.sum(jnp.where(pick, dots, 0.0), 1, keepdims=True)
+        result = jnp.where(place == k, value, result)
+    rw_out[...] = result
+
+    def sent(copy):
+        copy.wait_send()
+
+    for arr in arrays:
+        each_own(arr, sent)
+
+        def settle(p, _):
+            pl.when(p != z)(lambda: each_column(arr, p, sent))
+            sent(wide(*arr, SIB, block(p, 1 - y, c)))
+            return 0
+
+        lax.fori_loop(0, 4, settle, 0)
+
+    def settle_sums(p, _):
+        sent(to_sib(p, 0))
+        sent(to_sib(p, 1))
+
+        def step(h, _):
+            sent(to_side(p, h))
+            pl.when(p > z)(lambda: sent(along(p, h, UP)))
+            pl.when(p < z)(lambda: sent(along(p, h, DOWN)))
+            return 0
+
+        lax.fori_loop(0, PIECES, step, 0)
+        return 0
+
+    lax.fori_loop(0, 4, settle_sums, 0)
+
+
+def kernel_shards(tokens, out_grad, routes, route_weights, *matrices):
+    matrices = [matrix[0] for matrix in matrices]
+    rows, feat = tokens.shape
+    rank, hid = matrices[4].shape
+    wide = feat + LANES
+    plane = 4 * rows
+    shape = jax.ShapeDtypeStruct
+    vmem = pltpu.VMEM
+    sem = pltpu.SemaphoreType.DMA
+    outs = pl.pallas_call(
+        routed_kernel,
+        out_shape=(
+            shape((rows, feat), BF16),
+            shape(routes.shape, F32),
+            shape((rank, feat), F32),
+            shape((rank, hid), F32),
+            shape((rank, feat), F32),
+            shape((rank, hid), F32),
+            shape((rank, hid), F32),
+            shape((rank, feat), F32),
+        ),
+        in_specs=[pl.BlockSpec(memory_space=pltpu.VMEM)] * 13,
+        out_specs=tuple([pl.BlockSpec(memory_space=pltpu.VMEM)] * 8),
+        scratch_shapes=[
+            vmem((16 * rows, feat), BF16),
+            vmem((16 * rows, wide), BF16),
+            vmem((16 * rows, wide), BF16),
+            vmem((8 * rows, wide), BF16),
+            vmem((4 * rows, wide), BF16),
+            vmem((2, 4 * rows, wide), BF16),
+            vmem((LANES, feat), BF16),
+            vmem((LANES, 2 * hid), BF16),
+            vmem((LANES, hid), BF16),
+            vmem((LANES, feat), BF16),
+            vmem((plane, hid), F32),
+            vmem((plane, hid), F32),
+            vmem((plane, hid), F32),
+            vmem((plane, hid), BF16),
+            vmem((plane, hid), BF16),
+            vmem((plane, hid), BF16),
+            vmem((plane, LANES), BF16),
+            vmem((plane, LANES), F32),
+            vmem((plane, LANES), F32),
+            vmem((2 * rank, feat), F32),
+            vmem((2 * rank, 2 * hid), F32),
+            vmem((rank, hid), F32),
+            vmem((rank, feat), F32),
+            vmem((rows // PIECES, wide), F32),
+            sem((4, 16)), sem((16,)), sem((4, 16)), sem((16,)),
+            sem((8,)), sem((8,)),
+            sem((4, PIECES)), sem((4, PIECES)),
+            sem((4, PIECES)), sem((2, 4, PIECES)),
+        ],
+        compiler_params=pltpu.CompilerParams(
+            collective_id=0, has_side_effects=True, vmem_limit_bytes=60 * 1024 * 1024
+        ),
+        cost_estimate=pl.CostEstimate(
+            flops=12 * 16 * rows * feat * hid, bytes_accessed=6 * feat * hid + 8 * rows * feat,
+            transcendentals=16 * rows * hid,
+        ),
+    )(tokens, out_grad, routes, route_weights, *matrices)
+    return outs[:2] + tuple(out[None] for out in outs[2:])
 
 
 def slot_ranks(id_block, expert_count):
@@ -198,7 +637,7 @@
 
 def solution(mesh):
     return jax.shard_map(
-        shards,
+        kernel_shards if mesh.shape["expert"] == 16 else shards,
         mesh=mesh,
         in_specs=(
             P(("groups", "expert"), None),

time: 253 us -> 125 us (0.49)
  the two profiles are of different devices: /device:TPU:15 before, /device:TPU:0 now
where the time goes in v2:
time: 125 us; the launch traced here: 124 us
  Pallas kernels  109 us (87%)
  local copies, waits for them, and re-layouts  14.8 us (12%)
    pallas_call x1, Pallas kernels, kernel_shards(): pl.pallas_call(routed_kernel, out_shape=(shape((rows, feat), BF16), shape...  109 us
    unnamed x10, local copies, waits for them, and re-layouts  14.8 us

profile of v2, /device:TPU:0, one launch (start us, length us, event | category | flops | bytes accessed | tf_op | source)
XLA Modules:
  0.0 124.3 jit_solution(43459961895347727)
XLA Ops:
  0.6 1.4 %copy.22.weights_ref = bf16[64,8]{1,0:T(8,128)(2,1)} copy(bf16[64,8]{0,1:T(8,128)(2,1)} %param.16) | data formatting | bytes 2048 | tf_op args[3]
  2.0 1.4 %copy.21.routes_ref = s32[64,8]{1,0:T(8,128)} copy(s32[64,8]{0,1:T(8,128)} %param.15) | data formatting | bytes 4096 | tf_op args[2]
  3.4 108.8 %shard_map.188 = (bf16[64,2048]{1,0:T(8,128)(2,1)}, f32[64,8]{1,0:T(8,128)}, f32[16,2048]{1,0:T(8,128)}, f32[16,768]{1,0:T(8,128)}, f32[16,2048]{1,0:T(8,128)}, ...) custom-call(bf16[64,2048]{1,0:T(8,128)(2,1)} %x_ref.1, bf16[64,2048]{1,0:T(8,128)(2,1)} %g_ref.1, ...), custom_call_target="tpu_custom_call" | custom-call | flops 19327352832 | bytes 10485760 | tf_op jit(solution)/shard_map/pallas_call | solution.py:393
  112.2 1.4 %copy.23 = f32[64,8]{0,1:T(8,128)} copy(f32[64,8]{1,0:T(8,128)} %get-tuple-element.25) | data formatting | bytes 4096
  113.6 1.7 %copy.31 = bf16[64,2048]{1,0:T(8,128)(2,1)} copy(bf16[64,2048]{1,0:T(8,128)(2,1)} %get-tuple-element.40) | data formatting | bytes 524288
  115.3 1.6 %copy.32 = f32[1,16,2048]{2,1,0:T(8,128)} copy(f32[1,16,2048]{2,1,0:T(8,128)} %bitcast.17) | data formatting | bytes 262144
  116.9 1.4 %copy.33 = f32[1,16,768]{2,1,0:T(8,128)} copy(f32[1,16,768]{2,1,0:T(8,128)} %bitcast.20) | data formatting | bytes 98304
  118.3 1.6 %copy.34 = f32[1,16,2048]{2,1,0:T(8,128)} copy(f32[1,16,2048]{2,1,0:T(8,128)} %bitcast.16) | data formatting | bytes 262144
  119.9 1.4 %copy.35 = f32[1,16,768]{2,1,0:T(8,128)} copy(f32[1,16,768]{2,1,0:T(8,128)} %bitcast.19) | data formatting | bytes 98304
  121.3 1.4 %copy.36 = f32[1,16,768]{2,1,0:T(8,128)} copy(f32[1,16,768]{2,1,0:T(8,128)} %bitcast.18) | data formatting | bytes 98304
  122.7 1.6 %copy.37 = f32[1,16,2048]{2,1,0:T(8,128)} copy(f32[1,16,2048]{2,1,0:T(8,128)} %bitcast.15) | data formatting | bytes 262144

commit v3 on v2

--- a/solution.py
+++ b/solution.py
@@ -25,11 +25,11 @@
 
 
 def routed_kernel(
-    x_ref, g_ref, routes_ref, weights_ref, wg, wu, wd, gin, gout, uin, uout, din, dout,
+    x_ref, g_ref, routes_ref, weights_ref, wg_far, wu_far, wd_far, gin, gout, uin, uout, din, dout,
     tok_out, rw_out, ag_out, bg_out, au_out, bu_out, ad_out, bd_out,
     xbuf, gbuf, part, sbuf, ybuf, zbuf,
     ain, aout, dinp, doutp, gate_s, up_s, gh_s, hid_s, gg_s, gu_s, low_s, hlow_s, wcol_s,
-    acc_a, acc_b, acc_ad, acc_bd, total_s,
+    acc_a, acc_b, acc_ad, acc_bd, total_s, wg, wu, wd, wsem,
     xs, xr, gs, gr, ss, sr, ys, yr, zs, zr,
 ):
     rows, feat = x_ref.shape
@@ -72,8 +72,8 @@
     xbuf[own, :] = x_ref[...]
     gbuf[own, 0:feat] = g_ref[...]
     lane = lax.broadcasted_iota(jnp.int32, (rows, LANES), 1)
-    route = routes_ref[...]
-    route_w = weights_ref[...].astype(F32)
+    route = routes_ref[...].astype(F32).T.astype(jnp.int32)
+    route_w = weights_ref[...].astype(F32).T
     table = jnp.zeros((rows, LANES), F32)
     for k in range(route.shape[1]):
         table = jnp.where(lane == route[:, k : k + 1], route_w[:, k : k + 1], table)
@@ -129,6 +129,13 @@
 
     for arr in arrays:
         each_own(arr, start)
+
+    fetches = [
+        pltpu.make_async_copy(far, near, wsem.at[at])
+        for at, (far, near) in enumerate(((wg_far, wg), (wu_far, wu), (wd_far, wd)))
+    ]
+    for fetch in fetches:
+        fetch.start()
 
     ain[...] = jnp.zeros_like(ain)
     aout[...] = jnp.zeros_like(aout)
@@ -152,71 +159,53 @@
             ss.at[p * 2 + yy], sr.at[p * 2 + yy], SIB,
         )
 
-    def to_side(p, h):
+    def piece_at(p, yy, h):
+        return pl.ds((p * 2 + yy) * rows + h * piece, piece)
+
+    def to_side(h):
         return remote(
-            sbuf.at[pl.ds((p * 2 + 1 - y) * rows + h * piece, piece)],
-            ybuf.at[pl.ds(p * rows + h * piece, piece)],
-            ys.at[p, h], yr.at[p, h], SIDE,
+            sbuf.at[piece_at(z, 1 - y, h)], ybuf.at[pl.ds(h * piece, piece)],
+            ys.at[h], yr.at[h], SIDE,
         )
 
-    def along(p, h, kind):
+    def along(p, yy, h, kind):
         lead = 0 if kind == UP else 1
         return remote(
-            ybuf.at[pl.ds(p * rows + h * piece, piece)],
-            zbuf.at[lead, pl.ds(p * rows + h * piece, piece)],
-            zs.at[p, h], zr.at[lead, p, h], kind,
+            sbuf.at[piece_at(p, yy, h)], zbuf.at[lead, piece_at(p, yy, h)],
+            zs.at[p * 2 + yy, h], zr.at[lead, p * 2 + yy, h], kind,
         )
 
-    def sum_sib(p):
-        to_sib(p, 1 - y).wait_recv()
-
-        def step(h, _):
-            at = pl.ds((p * 2 + 1 - y) * rows + h * piece, piece)
-            mine = pl.ds(block(p, 1 - y, c) * rows + h * piece, piece)
-            sbuf[at, :] = (sbuf[at, :].astype(F32) + part[mine, :].astype(F32)).astype(BF16)
-            to_side(p, h).start()
-            return 0
-
-        lax.fori_loop(0, PIECES, step, 0)
-        to_sib(p, y).wait_recv()
-
-    def pair_sum(p, h):
-        to_side(p, h).wait_recv()
-        here = pl.ds(block(p, y, c) * rows + h * piece, piece)
-        near = pl.ds((p * 2 + y) * rows + h * piece, piece)
-        at = pl.ds(p * rows + h * piece, piece)
-        return part[here, :].astype(F32) + sbuf[near, :].astype(F32) + ybuf[at, :].astype(F32)
+    def wait_sums(p):
+        to_sib(p, 0).wait_recv()
+        to_sib(p, 1).wait_recv()
+
+    def chip_sum(p, yy, h):
+        here = pl.ds(block(p, yy, c) * rows + h * piece, piece)
+        total_s[...] = part[here, :].astype(F32) + sbuf[piece_at(p, yy, h), :].astype(F32)
+
+    def add_from(p, yy, h, kind):
+        along(p, yy, h, kind).wait_recv()
+        total_s[...] += zbuf[0 if kind == UP else 1, piece_at(p, yy, h), :].astype(F32)
 
     def pass_on(p, h):
-        at = pl.ds(p * rows + h * piece, piece)
-        ybuf[at, :] = pair_sum(p, h).astype(BF16)
-
-        @pl.when(p > z)
-        def _():
-            @pl.when(z > 0)
-            def _():
-                along(p, h, UP).wait_recv()
-                ybuf[at, :] = (ybuf[at, :].astype(F32) + zbuf[0, at, :].astype(F32)).astype(BF16)
-
-            along(p, h, UP).start()
-
-        @pl.when(p < z)
-        def _():
-            @pl.when(z < 3)
-            def _():
-                along(p, h, DOWN).wait_recv()
-                ybuf[at, :] = (ybuf[at, :].astype(F32) + zbuf[1, at, :].astype(F32)).astype(BF16)
-
-            along(p, h, DOWN).start()
+        for yy in (0, 1):
+            chip_sum(p, yy, h)
+            pl.when(jnp.logical_and(p > z, z > 0))(lambda: add_from(p, yy, h, UP))
+            pl.when(jnp.logical_and(p < z, z < 3))(lambda: add_from(p, yy, h, DOWN))
+            sbuf[piece_at(p, yy, h), :] = total_s[...].astype(BF16)
+            pl.when(p > z)(lambda: along(p, yy, h, UP).start())
+            pl.when(p < z)(lambda: along(p, yy, h, DOWN).start())
 
     def pass_all(p):
+        wait_sums(p)
+
         def step(h, _):
             pass_on(p, h)
             return 0
 
         lax.fori_loop(0, PIECES, step, 0)
 
-    chunk = 16
+    chunk = 64
     expert_lane = lax.broadcasted_iota(jnp.int32, (chunk, LANES), 1)
 
     def forward(p):
@@ -295,19 +284,22 @@
         relays(arrays[0], s)
         wait_sib(arrays[0], p)
         forward(p)
-        pl.when(s >= 1)(lambda: sum_sib(before))
+        pl.when(jnp.logical_and(inner == 0, s >= 2))(lambda: pass_all(before))
         relays(arrays[1], s)
         wait_sib(arrays[1], p)
         glow, lg = backward(p)
         to_sib(p, 0).start()
         to_sib(p, 1).start()
         outer(p, glow, lg)
-        pl.when(s >= 2 + inner)(lambda: pass_all(before))
+        pl.when(jnp.logical_and(inner == 1, s == 3))(lambda: pass_all(before))
         return 0
 
+    for fetch in fetches:
+        fetch.wait()
     lax.fori_loop(0, 4, body, 0)
     last = plane_at(3)
-    sum_sib(last)
+    wait_sums(last)
+    pl.when(inner == 1)(lambda: wait_sums(plane_at(1)))
 
     def tail(h, _):
         pass_on(last, h)
@@ -316,32 +308,36 @@
 
     lax.fori_loop(0, PIECES, tail, 0)
 
-    ag_out[...] = ADAPTER_SCALING * acc_a[0:rank, :]
-    au_out[...] = ADAPTER_SCALING * acc_a[rank : 2 * rank, :]
-    bg_out[...] = ADAPTER_SCALING * acc_b[0:rank, 0:hid]
-    bu_out[...] = ADAPTER_SCALING * acc_b[rank : 2 * rank, hid:]
-    ad_out[...] = ADAPTER_SCALING * acc_ad[...]
-    bd_out[...] = ADAPTER_SCALING * acc_bd[...]
+    ag_out[...] = acc_a[0:rank, :]
+    au_out[...] = acc_a[rank : 2 * rank, :]
+    bg_out[...] = acc_b[0:rank, 0:hid]
+    bu_out[...] = acc_b[rank : 2 * rank, hid:]
+    ad_out[...] = acc_ad[...]
+    bd_out[...] = acc_bd[...]
+
+    wait_sums(z)
+
+    def arrived(yy, h):
+        chip_sum(z, yy, h)
+        pl.when(z > 0)(lambda: add_from(z, yy, h, UP))
+        pl.when(z < 3)(lambda: add_from(z, yy, h, DOWN))
+
+    def cross(h, _):
+        arrived(1 - y, h)
+        sbuf[piece_at(z, 1 - y, h), :] = total_s[...].astype(BF16)
+        to_side(h).start()
+        return 0
 
     def finish(h, _):
-        at = pl.ds(z * rows + h * piece, piece)
-        total_s[...] = pair_sum(z, h)
-
-        @pl.when(z > 0)
-        def _():
-            along(z, h, UP).wait_recv()
-            total_s[...] += zbuf[0, at, :].astype(F32)
-
-        @pl.when(z < 3)
-        def _():
-            along(z, h, DOWN).wait_recv()
-            total_s[...] += zbuf[1, at, :].astype(F32)
-
-        ybuf[at, :] = total_s[...].astype(BF16)
+        arrived(y, h)
+        to_side(h).wait_recv()
+        at = pl.ds(h * piece, piece)
+        ybuf[at, :] = (total_s[...] + ybuf[at, :].astype(F32)).astype(BF16)
         return 0
 
+    lax.fori_loop(0, PIECES, cross, 0)
     lax.fori_loop(0, PIECES, finish, 0)
-    at = pl.ds(z * rows, rows)
+    at = pl.ds(0, rows)
     tok_out[...] = ybuf[at, 0:feat]
     dots = ybuf[at, feat:].astype(F32)
     place = lax.broadcasted_iota(jnp.int32, route.shape, 1)
@@ -350,7 +346,7 @@
         pick = jnp.logical_or(lane == route[:, k : k + 1], lane == route[:, k : k + 1] + 16)
         value = jnp.sum(jnp.where(pick, dots, 0.0), 1, keepdims=True)
         result = jnp.where(place == k, value, result)
-    rw_out[...] = result
+    rw_out[...] = result.T
 
     def sent(copy):
         copy.wait_send()
@@ -370,15 +366,26 @@
         sent(to_sib(p, 1))
 
         def step(h, _):
-            sent(to_side(p, h))
-            pl.when(p > z)(lambda: sent(along(p, h, UP)))
-            pl.when(p < z)(lambda: sent(along(p, h, DOWN)))
+            for yy in (0, 1):
+                pl.when(p > z)(lambda: sent(along(p, yy, h, UP)))
+                pl.when(p < z)(lambda: sent(along(p, yy, h, DOWN)))
             return 0
 
         lax.fori_loop(0, PIECES, step, 0)
         return 0
 
+    def settle_side(h, _):
+        sent(to_side(h))
+        return 0
+
+    lax.fori_loop(0, PIECES, settle_side, 0)
     lax.fori_loop(0, 4, settle_sums, 0)
+
+
+def hand_over(*refs):
+    for at in range(8):
+        value = refs[at][...]
+        refs[8 + at][...] = value if at < 2 else ADAPTER_SCALING * value
 
 
 def kernel_shards(tokens, out_grad, routes, route_weights, *matrices):
@@ -394,7 +401,7 @@
         routed_kernel,
         out_shape=(
             shape((rows, feat), BF16),
-            shape(routes.shape, F32),
+            shape(routes.shape[::-1], F32),
             shape((rank, feat), F32),
             shape((rank, hid), F32),
             shape((rank, feat), F32),
@@ -402,15 +409,17 @@
             shape((rank, hid), F32),
             shape((rank, feat), F32),
         ),
-        in_specs=[pl.BlockSpec(memory_space=pltpu.VMEM)] * 13,
+        in_specs=[pl.BlockSpec(memory_space=pltpu.VMEM)] * 4
+        + [pl.BlockSpec(memory_space=pl.ANY)] * 3
+        + [pl.BlockSpec(memory_space=pltpu.VMEM)] * 6,
         out_specs=tuple([pl.BlockSpec(memory_space=pltpu.VMEM)] * 8),
         scratch_shapes=[
             vmem((16 * rows, feat), BF16),
             vmem((16 * rows, wide), BF16),
             vmem((16 * rows, wide), BF16),
             vmem((8 * rows, wide), BF16),
-            vmem((4 * rows, wide), BF16),
-            vmem((2, 4 * rows, wide), BF16),
+            vmem((rows, wide), BF16),
+            vmem((2, 8 * rows, wide), BF16),
             vmem((LANES, feat), BF16),
             vmem((LANES, 2 * hid), BF16),
             vmem((LANES, hid), BF16),
@@ -429,10 +438,12 @@
             vmem((rank, hid), F32),
             vmem((rank, feat), F32),
             vmem((rows // PIECES, wide), F32),
+            vmem((feat, hid), BF16), vmem((feat, hid), BF16), vmem((hid, feat), BF16),
+            sem((3,)),
             sem((4, 16)), sem((16,)), sem((4, 16)), sem((16,)),
             sem((8,)), sem((8,)),
-            sem((4, PIECES)), sem((4, PIECES)),
-            sem((4, PIECES)), sem((2, 4, PIECES)),
+            sem((PIECES,)), sem((PIECES,)),
+            sem((8, PIECES)), sem((2, 8, PIECES)),
         ],
         compiler_params=pltpu.CompilerParams(
             collective_id=0, has_side_effects=True, vmem_limit_bytes=60 * 1024 * 1024
@@ -441,8 +452,14 @@
             flops=12 * 16 * rows * feat * hid, bytes_accessed=6 * feat * hid + 8 * rows * feat,
             transcendentals=16 * rows * hid,
         ),
-    )(tokens, out_grad, routes, route_weights, *matrices)
-    return outs[:2] + tuple(out[None] for out in outs[2:])
+    )(tokens, out_grad, routes.T, route_weights.T, *matrices)
+    outs = pl.pallas_call(
+        hand_over,
+        out_shape=tuple(shape(out.shape, out.dtype) for out in outs),
+        in_specs=[pl.BlockSpec(memory_space=pltpu.VMEM)] * 8,
+        out_specs=tuple([pl.BlockSpec(memory_space=pltpu.VMEM)] * 8),
+    )(*outs)
+    return (outs[0], outs[1].T) + tuple(out[None] for out in outs[2:])
 
 
 def slot_ranks(id_block, expert_count):

time: 125 us -> 111 us (0.89)
  local copies, waits for them, and re-layouts: 14.8 us -> 0 us
    unnamed x10 -> x0, local copies, waits for them, and re-layouts: 14.8 us -> none
    pallas_call x0 -> x1, Pallas kernels: none -> 2.09 us  [kernel_shards(): pl.pallas_call(hand_over, out_shape=tuple((shape(out.shape, out.dtype) fo...]
where the time goes in v3:
time: 111 us
  Pallas kernels  110 us (99%)
    pallas_call x1, Pallas kernels, kernel_shards(): pl.pallas_call(routed_kernel, out_shape=(shape((rows, feat), BF16), shape...  108 us

profile of v3, /device:TPU:0, one launch (start us, length us, event | category | flops | bytes accessed | tf_op | source)
XLA Modules:
  0.0 111.0 jit_solution(2810991102525268892)
XLA Ops:
  0.6 108.3 %shard_map.188 = (bf16[64,2048]{1,0:T(8,128)(2,1)}, f32[8,64]{1,0:T(8,128)}, f32[16,2048]{1,0:T(8,128)}, f32[16,768]{1,0:T(8,128)}, f32[16,2048]{1,0:T(8,128)}, ...) custom-call(bf16[64,2048]{1,0:T(8,128)(2,1)} %x_ref.1, bf16[64,2048]{1,0:T(8,128)(2,1)} %g_ref.1, ...), custom_call_target="tpu_custom_call" | custom-call | flops 19327352832 | bytes 10485760 | tf_op jit(solution)/shard_map/pallas_call | solution.py:400
  108.9 2.1 %shard_map.189 = (bf16[64,2048]{1,0:T(8,128)(2,1)}, f32[8,64]{1,0:T(8,128)}, f32[16,2048]{1,0:T(8,128)}, f32[16,768]{1,0:T(8,128)}, f32[16,2048]{1,0:T(8,128)}, ...) custom-call(bf16[64,2048]{1,0:T(8,128)(2,1)} %get-tuple-element.24.refs_0_, ...), custom_call_target="tpu_custom_call" | custom-call | tf_op jit(solution)/shard_map/pallas_call | solution.py:456

commit v4 on v3

--- a/solution.py
+++ b/solution.py
@@ -162,11 +162,29 @@
     def piece_at(p, yy, h):
         return pl.ds((p * 2 + yy) * rows + h * piece, piece)
 
-    def to_side(h):
+    def to_side(p, h):
         return remote(
-            sbuf.at[piece_at(z, 1 - y, h)], ybuf.at[pl.ds(h * piece, piece)],
-            ys.at[h], yr.at[h], SIDE,
+            sbuf.at[piece_at(p, 1 - y, h)], ybuf.at[pl.ds(p * rows + h * piece, piece)],
+            ys.at[p, h], yr.at[p, h], SIDE,
         )
+
+    def cross_first(p, h):
+        chip_sum(p, 1 - y, h)
+        sbuf[piece_at(p, 1 - y, h), :] = total_s[...].astype(BF16)
+        to_side(p, h).start()
+
+    def crossed(p, h):
+        to_side(p, h).wait_recv()
+        total_s[...] += ybuf[pl.ds(p * rows + h * piece, piece), :].astype(F32)
+
+    def pass_end(p, h):
+        chip_sum(p, y, h)
+        crossed(p, h)
+        pl.when(jnp.logical_and(p == 3, z > 0))(lambda: add_from(p, y, h, UP))
+        pl.when(jnp.logical_and(p == 0, z < 3))(lambda: add_from(p, y, h, DOWN))
+        sbuf[piece_at(p, y, h), :] = total_s[...].astype(BF16)
+        pl.when(p == 3)(lambda: along(p, y, h, UP).start())
+        pl.when(p == 0)(lambda: along(p, y, h, DOWN).start())
 
     def along(p, yy, h, kind):
         lead = 0 if kind == UP else 1
@@ -301,10 +319,34 @@
     wait_sums(last)
     pl.when(inner == 1)(lambda: wait_sums(plane_at(1)))
 
+    def tail_cross(h, _):
+        cross_first(last, h)
+        return 0
+
+    def tail_cross_near(h, _):
+        cross_first(plane_at(1), h)
+        return 0
+
     def tail(h, _):
-        pass_on(last, h)
-        pl.when(inner == 1)(lambda: pass_on(plane_at(1), h))
+        pass_end(last, h)
+        pl.when(inner == 1)(lambda: pass_end(plane_at(1), h))
         return 0
+
+    lax.fori_loop(0, PIECES, tail_cross, 0)
+
+    @pl.when(inner == 1)
+    def _():
+        lax.fori_loop(0, PIECES, tail_cross_near, 0)
+
+    wait_sums(z)
+
+    @pl.when(inner == 0)
+    def _():
+        def own_cross(h, _):
+            cross_first(z, h)
+            return 0
+
+        lax.fori_loop(0, PIECES, own_cross, 0)
 
     lax.fori_loop(0, PIECES, tail, 0)
 
@@ -315,8 +357,6 @@
     ad_out[...] = acc_ad[...]
     bd_out[...] = acc_bd[...]
 
-    wait_sums(z)
-
     def arrived(yy, h):
         chip_sum(z, yy, h)
         pl.when(z > 0)(lambda: add_from(z, yy, h, UP))
@@ -325,19 +365,21 @@
     def cross(h, _):
         arrived(1 - y, h)
         sbuf[piece_at(z, 1 - y, h), :] = total_s[...].astype(BF16)
-        to_side(h).start()
+        to_side(z, h).start()
         return 0
 
     def finish(h, _):
         arrived(y, h)
-        to_side(h).wait_recv()
-        at = pl.ds(h * piece, piece)
-        ybuf[at, :] = (total_s[...] + ybuf[at, :].astype(F32)).astype(BF16)
+        crossed(z, h)
+        ybuf[pl.ds(z * rows + h * piece, piece), :] = total_s[...].astype(BF16)
         return 0
 
-    lax.fori_loop(0, PIECES, cross, 0)
+    @pl.when(inner == 1)
+    def _():
+        lax.fori_loop(0, PIECES, cross, 0)
+
     lax.fori_loop(0, PIECES, finish, 0)
-    at = pl.ds(0, rows)
+    at = pl.ds(z * rows, rows)
     tok_out[...] = ybuf[at, 0:feat]
     dots = ybuf[at, feat:].astype(F32)
     place = lax.broadcasted_iota(jnp.int32, route.shape, 1)
@@ -365,20 +407,19 @@
         sent(to_sib(p, 0))
         sent(to_sib(p, 1))
 
+        end = 1 - (p % 3 + 1) // 2
+
         def step(h, _):
             for yy in (0, 1):
-                pl.when(p > z)(lambda: sent(along(p, yy, h, UP)))
-                pl.when(p < z)(lambda: sent(along(p, yy, h, DOWN)))
+                used = jnp.logical_or(end == 0, yy == y)
+                pl.when(jnp.logical_and(used, p > z))(lambda: sent(along(p, yy, h, UP)))
+                pl.when(jnp.logical_and(used, p < z))(lambda: sent(along(p, yy, h, DOWN)))
+            pl.when(jnp.logical_or(end == 1, p == z))(lambda: sent(to_side(p, h)))
             return 0
 
         lax.fori_loop(0, PIECES, step, 0)
         return 0
 
-    def settle_side(h, _):
-        sent(to_side(h))
-        return 0
-
-    lax.fori_loop(0, PIECES, settle_side, 0)
     lax.fori_loop(0, 4, settle_sums, 0)
 
 
@@ -418,7 +459,7 @@
             vmem((16 * rows, wide), BF16),
             vmem((16 * rows, wide), BF16),
             vmem((8 * rows, wide), BF16),
-            vmem((rows, wide), BF16),
+            vmem((4 * rows, wide), BF16),
             vmem((2, 8 * rows, wide), BF16),
             vmem((LANES, feat), BF16),
             vmem((LANES, 2 * hid), BF16),
@@ -442,7 +483,7 @@
             sem((3,)),
             sem((4, 16)), sem((16,)), sem((4, 16)), sem((16,)),
             sem((8,)), sem((8,)),
-            sem((PIECES,)), sem((PIECES,)),
+            sem((4, PIECES)), sem((4, PIECES)),
             sem((8, PIECES)), sem((2, 8, PIECES)),
         ],
         compiler_params=pltpu.CompilerParams(

time: 111 us -> 105 us (0.946)
  Pallas kernels: 110 us -> 103 us
    pallas_call x1, Pallas kernels: 108 us -> 101 us  [kernel_shards(): pl.pallas_call(routed_kernel, out_shape=(shape((rows, feat), BF16), shape...]
where the time goes in v4:
time: 105 us; the launch traced here: 104 us
  Pallas kernels  103 us (98%)
    pallas_call x1, Pallas kernels, kernel_shards(): pl.pallas_call(routed_kernel, out_shape=(shape((rows, feat), BF16), shape...  101 us

profile of v4, /device:TPU:0, one launch (start us, length us, event | category | flops | bytes accessed | tf_op | source)
XLA Modules:
  0.0 104.0 jit_solution(13878562057136995027)
XLA Ops:
  0.6 101.2 %shard_map.188 = (bf16[64,2048]{1,0:T(8,128)(2,1)}, f32[8,64]{1,0:T(8,128)}, f32[16,2048]{1,0:T(8,128)}, f32[16,768]{1,0:T(8,128)}, f32[16,2048]{1,0:T(8,128)}, ...) custom-call(bf16[64,2048]{1,0:T(8,128)(2,1)} %x_ref.1, bf16[64,2048]{1,0:T(8,128)(2,1)} %g_ref.1, ...), custom_call_target="tpu_custom_call" | custom-call | flops 19327352832 | bytes 10485760 | tf_op jit(solution)/shard_map/pallas_call | solution.py:441
  101.9 2.1 %shard_map.189 = (bf16[64,2048]{1,0:T(8,128)(2,1)}, f32[8,64]{1,0:T(8,128)}, f32[16,2048]{1,0:T(8,128)}, f32[16,768]{1,0:T(8,128)}, f32[16,2048]{1,0:T(8,128)}, ...) custom-call(bf16[64,2048]{1,0:T(8,128)(2,1)} %get-tuple-element.24.refs_0_, ...), custom_call_target="tpu_custom_call" | custom-call | tf_op jit(solution)/shard_map/pallas_call | solution.py:497
